TPU v7x, 32 devices: a whole 2x2x4 slice. The times are simulated.
32 devices in a mesh: ctx: 16 (over z, x, core), tp: 2 (over y).
Axes of the slice: x: 2, y: 2, z: 4, core: 2. Of those that a mesh axis runs over, the one named last changes fastest.
Arguments:
- qkv_in: bfloat16 [2048, 3, 4096], P('ctx', None, 'tp'), may hold values from -6 to 6
- short_taps: float32 [3, 3, 4096], P(None, None, 'tp'), may hold values from -3.5 to 3.5
- long_filter: float32 [2048, 4096], P('ctx', 'tp'), may hold values from -1.7 to 1.7
- skip_gain: float32 [4096], P('tp'), may hold values from 0.2 to 1.5
- out_weight: bfloat16 [4096, 4096], P('tp', 'ctx'), may hold values from -0.125 to 0.125
Outputs:
- mixed_out: bfloat16 [2048, 4096], P('ctx', 'tp')
All inputs are finite; a program needn't handle non-finite values.
Results may differ from a plain program's by a relative error of at most 0.0049.
Values may be sent and summed in bfloat16 or wider, within the bound.
No kernel may reach another device: no remote copies, remote signals or barrier semaphores. Data moves between devices by JAX's collectives and lax.ppermute only.
A program may use at most 128 MiB of HBM per device.

v0:
```python
import math

import jax
import jax.numpy as jnp
from jax import lax
from jax.sharding import PartitionSpec as P

highest = lax.Precision.HIGHEST


def from_behind(value, axis, by):
    length = lax.axis_size(axis)
    pairs = [(i, i + by) for i in range(length) if 0 <= i + by < length]
    return lax.ppermute(value, axis, pairs)


def angles(count_rows, count_cols, offset, period, direction):
    row_ids = lax.iota(jnp.int32, count_rows)[:, None]
    col_ids = lax.iota(jnp.int32, count_cols)[None, :] + offset
    phase_int = row_ids * col_ids % period
    radians = phase_int.astype(jnp.float32) * (direction * 2.0 * math.pi / period)
    return (jnp.cos(radians), jnp.sin(radians))


def across_forward(signal, peer_count):
    cos_table, sin_table = angles(2 * peer_count, peer_count, 0, 2 * peer_count, -1.0)
    real_part = jnp.dot(cos_table, signal, precision=highest, preferred_element_type=jnp.float32)
    imag_part = jnp.dot(sin_table, signal, precision=highest, preferred_element_type=jnp.float32)
    return (real_part, imag_part)


def across_inverse(real_part, imag_part, peer_count):
    cos_table, sin_table = angles(peer_count, 2 * peer_count, 0, 2 * peer_count, 1.0)
    first_term = jnp.dot(
        cos_table, real_part, precision=highest, preferred_element_type=jnp.float32
    )
    second_term = jnp.dot(
        sin_table, imag_part, precision=highest, preferred_element_type=jnp.float32
    )
    return first_term - second_term


def rotate(real_part, imag_part, offset, total_len, direction):
    cos_table, sin_table = angles(
        real_part.shape[0], real_part.shape[1], offset, total_len, direction
    )
    cos_table = cos_table[:, :, None]
    sin_table = sin_table[:, :, None]
    return (
        real_part * cos_table - imag_part * sin_table,
        real_part * sin_table + imag_part * cos_table,
    )


def contract(matrix, operand):
    return jnp.einsum("ki,aic->akc", matrix, operand, precision=highest)


def along_rows(real_part, imag_part, direction):
    row_count = real_part.shape[1]
    cos_table, sin_table = angles(row_count, row_count, 0, row_count, direction)
    new_real = contract(cos_table, real_part) - contract(sin_table, imag_part)
    new_imag = contract(cos_table, imag_part) + contract(sin_table, real_part)
    return (new_real, new_imag)


def multiply(left_pair, right_pair):
    return (
        left_pair[0] * right_pair[0] - left_pair[1] * right_pair[1],
        left_pair[0] * right_pair[1] + left_pair[1] * right_pair[0],
    )


def over_slabs(mixed_in, long_filter):
    peer_count = lax.axis_size("ctx")
    position = lax.axis_index("ctx")
    row_count, channel_count = mixed_in.shape
    block_rows = row_count // peer_count
    total_len = 2 * peer_count * row_count
    pieces_in = (
        lax.all_to_all(mixed_in[None], "ctx", split_axis=1, concat_axis=0, tiled=True),
        lax.all_to_all(long_filter[None], "ctx", split_axis=1, concat_axis=0, tiled=True),
    )
    halves = []
    for received in pieces_in:
        real_part, imag_part = across_forward(
            received.reshape(peer_count, block_rows * channel_count), peer_count
        )
        cube_shape = (2 * peer_count, block_rows, channel_count)
        halves.append(
            rotate(
                real_part.reshape(cube_shape),
                imag_part.reshape(cube_shape),
                position * block_rows,
                total_len,
                -1.0,
            )
        )
    shuffled = (
        lax.all_to_all(halves[0][0], "ctx", split_axis=0, concat_axis=1, tiled=True),
        lax.all_to_all(halves[0][1], "ctx", split_axis=0, concat_axis=1, tiled=True),
        lax.all_to_all(halves[1][0], "ctx", split_axis=0, concat_axis=1, tiled=True),
        lax.all_to_all(halves[1][1], "ctx", split_axis=0, concat_axis=1, tiled=True),
    )
    signal_freq = along_rows(shuffled[0], shuffled[1], -1.0)
    filter_freq = along_rows(shuffled[2], shuffled[3], -1.0)
    product_pair = multiply(signal_freq, filter_freq)
    back_real, back_imag = along_rows(product_pair[0], product_pair[1], 1.0)
    returned = (
        lax.all_to_all(back_real, "ctx", split_axis=1, concat_axis=0, tiled=True),
        lax.all_to_all(back_imag, "ctx", split_axis=1, concat_axis=0, tiled=True),
    )
    turned_real, turned_imag = rotate(
        returned[0], returned[1], position * block_rows, total_len, 1.0
    )
    flat_shape = (2 * peer_count, block_rows * channel_count)
    output = across_inverse(
        turned_real.reshape(flat_shape), turned_imag.reshape(flat_shape), peer_count
    ) * (1.0 / total_len)
    settled = lax.all_to_all(
        output.reshape(peer_count, block_rows, channel_count),
        "ctx",
        split_axis=0,
        concat_axis=1,
        tiled=True,
    )
    return settled.reshape(row_count, channel_count)


def body(qkv_in, short_taps, long_filter, skip_gain, out_weight):
    row_count = qkv_in.shape[0]
    tap_count = short_taps.shape[1]
    last_rows = qkv_in[row_count - (tap_count - 1) :]
    earlier = from_behind(last_rows, "ctx", 1)
    extended = jnp.concatenate([earlier, qkv_in], axis=0).astype(jnp.float32)
    featured = short_taps[:, 0, :][None] * extended[tap_count - 1 : tap_count - 1 + row_count]
    for index_tap in range(1, tap_count):
        begin = tap_count - 1 - index_tap
        featured = (
            featured + short_taps[:, index_tap, :][None] * extended[begin : begin + row_count]
        )
    queries = featured[:, 0, :]
    mixed_in = featured[:, 1, :] * featured[:, 2, :]
    convolved = over_slabs(mixed_in, long_filter)
    gated_rows = (queries * (convolved + skip_gain[None, :] * mixed_in)).astype(jnp.bfloat16)
    partials = jnp.dot(
        gated_rows,
        lax.all_gather(out_weight, "ctx", axis=1, tiled=True),
        preferred_element_type=jnp.float32,
    )
    return lax.psum_scatter(partials, "tp", scatter_dimension=1, tiled=True).astype(jnp.bfloat16)


def solution(mesh):
    return jax.shard_map(
        body,
        mesh=mesh,
        in_specs=(
            P("ctx", None, "tp"),
            P(None, None, "tp"),
            P("ctx", "tp"),
            P("tp"),
            P("tp", "ctx"),
        ),
        out_specs=P("ctx", "tp"),
        check_vma=False,
    )
```

profile of v0, /device:TPU:5, one launch (start us, length us, event | category | flops | bytes accessed | tf_op | source)
XLA Modules:
  0.0 605.0 jit_solution(17149773485793183957)
XLA Ops:
  6.5 0.9 slice.31
  7.5 3.8 collective-permute-start
  11.3 2.9 broadcast_in_dim.2
  14.2 5.0 all-to-all-start.3
  19.4 0.5 maximum_convert_fusion
  19.8 0.9 fusion.1
  20.8 0.2 fusion.200
  21.0 1.4 copy-done.3
  22.4 2.6 copy_multiply_fusion
  25.0 17.4 %all-to-all-done.3 = f32[1,128,2048]{2,0,1:T(1,128)S(1)} async-done(((f32[1,128,2048]{2,0,1:T(1,128)}), f32[1,128,2048]{2,0,1:T(1,128)S(1)}, u32[]{:S(2)}, u32[]{:S(2)}) %all-to-all-start.3) | async-done | bytes 1048608 | tf_op jit(solution)/shard_map/all_to_all | solution.py:82
  42.3 6.7 %all-to-all-start = ((f32[1,128,2048]{2,0,1:T(1,128)}), f32[1,128,2048]{2,0,1:T(1,128)S(1)}, u32[]{:S(2)}, u32[]{:S(2)}) async-start(f32[1,128,2048]{2,0,1:T(1,128)} %bitcast.2), calls=%async_computation | async-start | bytes 2097152 | tf_op jit(solution)/shard_map/all_to_all | solution.py:81
  49.2 0.5 all-gather.2.cloned.1.call-update
  49.9 2.5 reduce.1
  52.6 3.2 fusion.40
  55.8 25.6 %all-to-all-done = f32[1,128,2048]{2,0,1:T(1,128)S(1)} async-done(((f32[1,128,2048]{2,0,1:T(1,128)}), f32[1,128,2048]{2,0,1:T(1,128)S(1)}, u32[]{:S(2)}, u32[]{:S(2)}) %all-to-all-start) | async-done | bytes 1048608 | tf_op jit(solution)/shard_map/all_to_all | solution.py:81
  81.4 2.5 reduce
  84.1 1.9 fusion.42
  86.0 1.9 fusion.44
  87.9 4.8 multiply_add_fusion.1
  92.7 2.6 copy.72
  95.3 15.9 %all-to-all-start.4 = ((f32[32,8,2048]{2,1,0:T(8,128)}), f32[32,8,2048]{2,1,0:T(8,128)S(1)}, u32[]{:S(2)}, u32[]{:S(2)}) async-start(f32[32,8,2048]{2,1,0:T(8,128)} %copy.72), calls=%async_computation.4 | async-start | bytes 4194304 | tf_op jit(solution)/shard_map/all_to_all | solution.py:102
  111.2 4.1 copy.75
  115.3 73.4 %all-to-all-done.4 = f32[32,8,2048]{2,1,0:T(8,128)S(1)} async-done(((f32[32,8,2048]{2,1,0:T(8,128)}), f32[32,8,2048]{2,1,0:T(8,128)S(1)}, u32[]{:S(2)}, u32[]{:S(2)}) %all-to-all-start.4) | async-done | bytes 2097184 | tf_op jit(solution)/shard_map/all_to_all | solution.py:102
  188.7 29.5 %all-to-all-start.5 = ((f32[32,8,2048]{2,1,0:T(8,128)}), f32[32,8,2048]{2,1,0:T(8,128)}, u32[]{:S(2)}, u32[]{:S(2)}) async-start(f32[32,8,2048]{2,1,0:T(8,128)} %copy.75), calls=%async_computation.5 | async-start | bytes 4194304 | tf_op jit(solution)/shard_map/all_to_all | solution.py:103
  218.3 4.2 copy.64
  222.5 42.5 %all-to-all-done.5 = f32[32,8,2048]{2,1,0:T(8,128)} async-done(((f32[32,8,2048]{2,1,0:T(8,128)}), f32[32,8,2048]{2,1,0:T(8,128)}, u32[]{:S(2)}, u32[]{:S(2)}) %all-to-all-start.5) | async-done | bytes 2097184 | tf_op jit(solution)/shard_map/all_to_all | solution.py:103
  264.9 11.3 %all-to-all-start.1 = ((f32[32,8,2048]{2,1,0:T(8,128)}), f32[32,8,2048]{2,1,0:T(8,128)}, u32[]{:S(2)}, u32[]{:S(2)}) async-start(f32[32,8,2048]{2,1,0:T(8,128)} %copy.64), calls=%async_computation.1 | async-start | bytes 4194304 | tf_op jit(solution)/shard_map/all_to_all | solution.py:100
  276.2 4.1 copy.67
  280.3 37.5 %all-to-all-done.1 = f32[32,8,2048]{2,1,0:T(8,128)} async-done(((f32[32,8,2048]{2,1,0:T(8,128)}), f32[32,8,2048]{2,1,0:T(8,128)}, u32[]{:S(2)}, u32[]{:S(2)}) %all-to-all-start.1) | async-done | bytes 2097184 | tf_op jit(solution)/shard_map/all_to_all | solution.py:100
  317.8 11.2 %all-to-all-start.2 = ((f32[32,8,2048]{2,1,0:T(8,128)}), f32[32,8,2048]{2,1,0:T(8,128)}, u32[]{:S(2)}, u32[]{:S(2)}) async-start(f32[32,8,2048]{2,1,0:T(8,128)} %copy.67), calls=%async_computation.2 | async-start | bytes 4194304 | tf_op jit(solution)/shard_map/all_to_all | solution.py:101
  329.0 4.8 fusion.15
  333.9 6.5 %fusion.21 = f32[2,2048,128]{2,1,0:T(8,128)} fusion(f32[2,16,8,2048]{3,2,0,1:T(8,128)} %bitcast.6), kind=kOutput, calls=%fused_computation.31 | convolution fusion | flops 805535744 | bytes 4194304 | tf_op jit(solution)/shard_map/ki,aic->akc/dot_general | solution.py:56
  340.4 6.5 %fusion.11 = f32[2,2048,128]{2,1,0:T(8,128)} fusion(f32[2,16,8,2048]{3,2,0,1:T(8,128)} %bitcast.18), kind=kOutput, calls=%fused_computation.21 | convolution fusion | flops 805535744 | bytes 4194304 | tf_op jit(solution)/shard_map/ki,aic->akc/dot_general | solution.py:56
  346.9 23.3 %all-to-all-done.2 = f32[32,8,2048]{2,1,0:T(8,128)} async-done(((f32[32,8,2048]{2,1,0:T(8,128)}), f32[32,8,2048]{2,1,0:T(8,128)}, u32[]{:S(2)}, u32[]{:S(2)}) %all-to-all-start.2) | async-done | bytes 2097184 | tf_op jit(solution)/shard_map/all_to_all | solution.py:101
  370.2 5.5 fusion.17
  375.7 5.3 convolution_subtract_fusion.2
  381.0 5.3 convolution_subtract_fusion.3
  386.3 4.0 convolution_add_fusion.1
  390.3 5.3 multiply_subtract_fusion
  395.6 2.1 fusion.9
  397.8 3.4 fusion.4
  401.2 4.2 copy.82
  405.4 10.9 %all-to-all-start.6 = ((f32[2,128,2048]{2,0,1:T(2,128)}), f32[2,128,2048]{2,0,1:T(2,128)}, u32[]{:S(2)}, u32[]{:S(2)}) async-start(f32[2,128,2048]{2,0,1:T(2,128)} %copy.82), calls=%async_computation.6 | async-start | bytes 4194304 | tf_op jit(solution)/shard_map/all_to_all | solution.py:110
  416.3 3.7 fusion.5
  420.0 3.4 fusion.3
  423.4 4.2 copy.86
  427.6 30.2 %all-to-all-done.6 = f32[2,128,2048]{2,0,1:T(2,128)} async-done(((f32[2,128,2048]{2,0,1:T(2,128)}), f32[2,128,2048]{2,0,1:T(2,128)}, u32[]{:S(2)}, u32[]{:S(2)}) %all-to-all-start.6) | async-done | bytes 2097184 | tf_op jit(solution)/shard_map/all_to_all | solution.py:110
  457.9 10.9 %all-to-all-start.7 = ((f32[2,128,2048]{2,0,1:T(2,128)}), f32[2,128,2048]{2,0,1:T(2,128)}, u32[]{:S(2)}, u32[]{:S(2)}) async-start(f32[2,128,2048]{2,0,1:T(2,128)} %copy.86), calls=%async_computation.7 | async-start | bytes 4194304 | tf_op jit(solution)/shard_map/all_to_all | solution.py:111
  469.2 1.2 copy.105
  470.7 2.5 copy.107
  473.3 2.8 copy.171
  476.3 2.6 copy.104
  478.8 31.4 %all-to-all-done.7 = f32[2,128,2048]{2,0,1:T(2,128)} async-done(((f32[2,128,2048]{2,0,1:T(2,128)}), f32[2,128,2048]{2,0,1:T(2,128)}, u32[]{:S(2)}, u32[]{:S(2)}) %all-to-all-start.7) | async-done | bytes 2097184 | tf_op jit(solution)/shard_map/all_to_all | solution.py:111
  510.3 2.8 copy.170
  513.3 1.2 copy.106
  514.6 0.4 copy-done.1
  514.9 0.6 copy-done.2
  515.5 1.5 fusion.26
  517.0 1.5 fusion
  518.5 0.6 copy.108
  519.2 35.9 %all_to_all.135 = f32[16,8,2048]{2,1,0:T(8,128)S(1)} all-to-all(f32[16,8,2048]{2,1,0:T(8,128)S(1)} %bitcast.175), channel_id=1, replica_groups=mesh['ctx'=16,'tp'=2] {'ctx'}, dimensions={0} | all-to-all | bytes 2097152 | tf_op jit(solution)/shard_map/all_to_all | solution.py:120
  555.0 10.4 %fusion.53 = f32[128,4096]{1,0:T(8,128)} fusion(bf16[2048,4096]{1,0:T(8,128)(2,1)} %all-gather.2.cloned.1.call-done, f32[128,3,2048]{2,0,1:T(8,128)} %copy-done.3, f32[128,1,2048]{2,1,0:T(1,128)} %copy_multiply_fusion, f32[16,8,2048]{2,1,0:T(8,128)S(1)} %all_to_all.135, f32[2048]{0:T(1024)S(1)} %copy-done.9), kind=kOutput, calls=%fused_computation.75 | convolution fusion | flops 2148532224 | bytes 22028288 | tf_op jit(solution)/shard_map/dot_general | solution.py:146
  565.5 30.3 %reduce-scatter.2.cloned.1.call-done = f32[128,2048]{1,0:T(8,128)} async-done(((f32[128,4096]{1,0:T(8,128)}), f32[128,2048]{1,0:T(8,128)}) %reduce-scatter.2.cloned.1.call-update) | async-done | bytes 1048592 | tf_op jit(solution)/shard_map/reduce_scatter | solution.py:151
  595.8 2.1 convert_element_type.75
  (37 shorter events, 2.1 us)
Async XLA Ops:
  7.5 11.8 %copy-start.10 = (f32[3,3,2048]{2,1,0:T(4,128)S(1)}, f32[3,3,2048]{2,1,0:T(4,128)}, u32[]{:S(2)}) copy-start(f32[3,3,2048]{2,1,0:T(4,128)} %param.6) | copy-start | bytes 221188
  7.5 11.9 %copy-start.8 = (bf16[128,3,2048]{2,0,1:T(8,128)(2,1)S(1)}, bf16[128,3,2048]{2,0,1:T(8,128)(2,1)}, u32[]{:S(2)}) copy-start(bf16[128,3,2048]{2,0,1:T(8,128)(2,1)} %param.5) | copy-start | bytes 4718596
  7.5 11.9 %collective-permute-start = (bf16[2,3,2048]{2,0,1:T(2,128)(2,1)S(1)}, bf16[2,3,2048]{2,0,1:T(2,128)(2,1)S(1)}, u32[]{:S(2)}, u32[]{:S(2)}) collective-permute-start(bf16[2,3,2048]{2,0,1:T(2,128)(2,1)S(1)} %slice.31), channel_id=1, source_target_pairs={{0,2},{2,4},{4,6},{6,8},{8,10},{10,12},{12,14},{14,16},{16,18},{18... | collective-permute-start | bytes 73736 | tf_op jit(solution)/shard_map/ppermute | solution.py:14
  14.2 28.1 %all-to-all-start.3 = ((f32[1,128,2048]{2,0,1:T(1,128)}), f32[1,128,2048]{2,0,1:T(1,128)S(1)}, u32[]{:S(2)}, u32[]{:S(2)}) async-start(f32[1,128,2048]{2,0,1:T(1,128)} %broadcast_in_dim.2), calls=%async_computation.3 | async-start | bytes 2097152 | tf_op jit(solution)/shard_map/all_to_all | solution.py:82
  20.8 1.6 copy-start.3
  42.3 39.0 %all-to-all-start = ((f32[1,128,2048]{2,0,1:T(1,128)}), f32[1,128,2048]{2,0,1:T(1,128)S(1)}, u32[]{:S(2)}, u32[]{:S(2)}) async-start(f32[1,128,2048]{2,0,1:T(1,128)} %bitcast.2), calls=%async_computation | async-start | bytes 2097152 | tf_op jit(solution)/shard_map/all_to_all | solution.py:81
  49.0 506.0 %all-gather.2.cloned.1.call-start = ((), (), s32[]{:S(2)}) async-start(), calls=%async_computation.10 | async-start | bytes 17825792 | tf_op jit(solution)/shard_map/all_gather | solution.py:148
  86.0 1.9 copy-start.4
  95.3 93.4 %all-to-all-start.4 = ((f32[32,8,2048]{2,1,0:T(8,128)}), f32[32,8,2048]{2,1,0:T(8,128)S(1)}, u32[]{:S(2)}, u32[]{:S(2)}) async-start(f32[32,8,2048]{2,1,0:T(8,128)} %copy.72), calls=%async_computation.4 | async-start | bytes 4194304 | tf_op jit(solution)/shard_map/all_to_all | solution.py:102
  188.7 76.2 %all-to-all-start.5 = ((f32[32,8,2048]{2,1,0:T(8,128)}), f32[32,8,2048]{2,1,0:T(8,128)}, u32[]{:S(2)}, u32[]{:S(2)}) async-start(f32[32,8,2048]{2,1,0:T(8,128)} %copy.75), calls=%async_computation.5 | async-start | bytes 4194304 | tf_op jit(solution)/shard_map/all_to_all | solution.py:103
  264.9 52.9 %all-to-all-start.1 = ((f32[32,8,2048]{2,1,0:T(8,128)}), f32[32,8,2048]{2,1,0:T(8,128)}, u32[]{:S(2)}, u32[]{:S(2)}) async-start(f32[32,8,2048]{2,1,0:T(8,128)} %copy.64), calls=%async_computation.1 | async-start | bytes 4194304 | tf_op jit(solution)/shard_map/all_to_all | solution.py:100
  317.8 52.4 %all-to-all-start.2 = ((f32[32,8,2048]{2,1,0:T(8,128)}), f32[32,8,2048]{2,1,0:T(8,128)}, u32[]{:S(2)}, u32[]{:S(2)}) async-start(f32[32,8,2048]{2,1,0:T(8,128)} %copy.67), calls=%async_computation.2 | async-start | bytes 4194304 | tf_op jit(solution)/shard_map/all_to_all | solution.py:101
  370.2 5.5 copy-start.7
  375.7 5.3 copy-start.6
  381.0 5.3 copy-start.5
  395.6 2.2 copy-start
  405.4 52.4 %all-to-all-start.6 = ((f32[2,128,2048]{2,0,1:T(2,128)}), f32[2,128,2048]{2,0,1:T(2,128)}, u32[]{:S(2)}, u32[]{:S(2)}) async-start(f32[2,128,2048]{2,0,1:T(2,128)} %copy.82), calls=%async_computation.6 | async-start | bytes 4194304 | tf_op jit(solution)/shard_map/all_to_all | solution.py:110
  457.9 52.4 %all-to-all-start.7 = ((f32[2,128,2048]{2,0,1:T(2,128)}), f32[2,128,2048]{2,0,1:T(2,128)}, u32[]{:S(2)}, u32[]{:S(2)}) async-start(f32[2,128,2048]{2,0,1:T(2,128)} %copy.86), calls=%async_computation.7 | async-start | bytes 4194304 | tf_op jit(solution)/shard_map/all_to_all | solution.py:111
  468.7 127.1 %reduce-scatter.2.cloned.1.call-start = ((), (), s32[]{:S(2)}) async-start(), calls=%async_computation.11 | async-start | bytes 3145728 | tf_op jit(solution)/shard_map/reduce_scatter | solution.py:151
  513.3 1.6 copy-start.1
  513.3 2.2 copy-start.2
  518.5 36.5 %copy-start.9 = (f32[2048]{0:T(1024)S(1)}, f32[2048]{0:T(1024)}, u32[]{:S(2)}) copy-start(f32[2048]{0:T(1024)} %param.8) | copy-start | bytes 24580
Sparse Core Ops, SparseCore 0:
  52.0 197.3 all-gather.1
  565.6 30.1 reduce-scatter.1
where the time goes:
time: 613 us; the launch traced here: 605 us
  waiting for transfers between devices  312 us (51%)
  starting transfers between devices  106 us (17%)
  matrix products  81.1 us (13%)
  local copies, waits for them, and re-layouts  45.2 us (7%)
  blocking collectives  35.9 us (6%)
  between operations  14 us (2%)
  other arithmetic  11.2 us (2%)
    all_to_all x1, waiting for transfers between devices, over_slabs(): lax.all_to_all(halves[1][0], 'ctx', split_axis=0, concat_axis=1, tiled=True)  73.4 us
    dot_general x12, matrix products, contract(): return jnp.einsum('ki,aic->akc', matrix, operand, precision=highest)  55.8 us
    all_to_all x1, waiting for transfers between devices, over_slabs(): lax.all_to_all(halves[1][1], 'ctx', split_axis=0, concat_axis=1, tiled=True)  42.5 us
    all_to_all x1, waiting for transfers between devices, over_slabs(): lax.all_to_all(halves[0][0], 'ctx', split_axis=0, concat_axis=1, tiled=True)  37.5 us
    all_to_all x1, blocking collectives, over_slabs(): lax.all_to_all(output.reshape(peer_count, block_rows, channel_count), 'ct...  35.9 us
    all_to_all x1, waiting for transfers between devices, over_slabs(): lax.all_to_all(back_imag, 'ctx', split_axis=1, concat_axis=0, tiled=True)  31.4 us
    reduce_scatter x1, waiting for transfers between devices, body(): lax.psum_scatter(partials, 'tp', scatter_dimension=1, tiled=True)  30.3 us
    all_to_all x1, waiting for transfers between devices, over_slabs(): lax.all_to_all(back_real, 'ctx', split_axis=1, concat_axis=0, tiled=True)  30.2 us
  transfers between devices with their start and end apart: 11, of which 9 were waited for; matrix products, arithmetic and copies ran while one was open for 20% of the time, Pallas kernels for 0%

commit v1 on v0

v1 whole, which is shorter than its diff:
```python
import functools
import itertools

import jax
import jax.numpy as jnp
import numpy as np
from jax import lax
from jax.experimental import pallas as pl
from jax.experimental.pallas import tpu as pltpu
from jax.sharding import PartitionSpec as P

BLOCK = 256
ROWS_AT_ONCE = 8
EDGE_ROWS = 16


def split_bf16(matrix):
    high = matrix.astype(jnp.bfloat16)
    low = (matrix - high.astype(np.float64)).astype(jnp.bfloat16)
    return high, low


@functools.cache
def transform_tables(block):
    freq = np.arange(block)[:, None] + 0.5
    radians = np.pi * freq * np.arange(block)[None, :] / block
    table = np.concatenate([np.cos(radians), -np.sin(radians)], axis=0)
    high, low = split_bf16(table)
    back_high, back_low = split_bf16(table.T / block)
    forward = np.concatenate([high, low], axis=1)
    backward = np.concatenate([back_high, back_low, back_high], axis=1)
    return forward, backward


def blocks_together(lanes, count):
    return 2 if lanes % 128 == 0 and count % 2 == 0 else 1


def forward_into(table_ref, read, count, spectra):
    together = blocks_together(read(0).shape[1], count)
    for first in range(0, count, together):
        columns = [read(first + i) for i in range(together)]
        wide = jnp.concatenate(columns, axis=1) if together > 1 else columns[0]
        spectrum = jnp.dot(
            table_ref[...],
            jnp.concatenate([wide, wide], axis=0),
            preferred_element_type=jnp.float32,
        )
        lanes = columns[0].shape[1]
        for i in range(together):
            spectra[first + i] = spectrum[:, i * lanes : (i + 1) * lanes]


def conv_kernel(
    table_ref,
    back_ref,
    arrived_ref,
    taps_ref,
    skip_ref,
    out_ref,
    spectra,
    filter_ref,
    products,
    padded,
    mixed,
    edges,
):
    block = table_ref.shape[1] // 2
    slabs, _, lanes = arrived_ref.shape
    tokens = mixed.shape[0]
    slab_rows = tokens // slabs
    count = tokens // block
    per_block = block // slab_rows

    def reader(kind):
        begin = kind * slab_rows

        def read(index):
            part = arrived_ref[
                index * per_block : (index + 1) * per_block, begin : begin + slab_rows
            ]
            return part.reshape(block, lanes)

        return read

    for index in range(count):
        mixed[index * block : (index + 1) * block] = reader(2)(index).astype(jnp.float32)
    complete_mixed(arrived_ref, taps_ref, mixed, edges)

    def read_mixed(index):
        return mixed[index * block : (index + 1) * block].astype(jnp.bfloat16)

    forward_into(table_ref, read_mixed, count, spectra)
    forward_into(table_ref, reader(0), count, filter_ref)

    parity = lax.broadcasted_iota(jnp.int32, (block, lanes), 0) % 2
    sign = (1 - 2 * parity).astype(jnp.float32)
    for index in range(count - 1, 0, -1):
        before_real = filter_ref[index - 1, :block]
        before_imag = filter_ref[index - 1, block:]
        filter_ref[index, :block] = filter_ref[index, :block] - sign * before_imag
        filter_ref[index, block:] = filter_ref[index, block:] + sign * before_real

    margin = padded.shape[0] - tokens
    padded[:margin] = jnp.zeros((margin, lanes), jnp.float32)
    for index in range(count):
        at = margin + index * block
        padded[at : at + block] = reader(1)(index).astype(jnp.float32)

    def rows_step(step, carry):
        at = pl.multiple_of(step * ROWS_AT_ONCE, ROWS_AT_ONCE)
        real_rows = pl.ds(at, ROWS_AT_ONCE)
        imag_rows = pl.ds(pl.multiple_of(block + at, ROWS_AT_ONCE), ROWS_AT_ONCE)
        signal_real = [spectra[i, real_rows] for i in range(count)]
        signal_imag = [spectra[i, imag_rows] for i in range(count)]
        filter_real = [filter_ref[i, real_rows] for i in range(count)]
        filter_imag = [filter_ref[i, imag_rows] for i in range(count)]
        for target in range(count):
            real = imag = None
            for source in range(target + 1):
                a, b = signal_real[source], signal_imag[source]
                c, d = filter_real[target - source], filter_imag[target - source]
                term_real = a * c - b * d
                term_imag = a * d + b * c
                real = term_real if real is None else real + term_real
                imag = term_imag if imag is None else imag + term_imag
            products[target, real_rows] = real
            products[target, imag_rows] = imag
        return carry

    def long_step(target, carry):
        def add(source, totals):
            a, b = spectra[source, :block], spectra[source, block:]
            c, d = filter_ref[target - source, :block], filter_ref[target - source, block:]
            return totals[0] + (a * c - b * d), totals[1] + (a * d + b * c)

        zero = jnp.zeros((block, lanes), jnp.float32)
        real, imag = lax.fori_loop(0, target + 1, add, (zero, zero))
        products[target, :block] = real
        products[target, block:] = imag
        return carry

    if count <= 8:
        lax.fori_loop(0, block // ROWS_AT_ONCE, rows_step, 0)
    else:
        lax.fori_loop(0, count, long_step, 0)

    together = blocks_together(lanes, count)
    for first in range(0, count, together):
        parts = [products[first + i] for i in range(together)]
        wide = jnp.concatenate(parts, axis=1) if together > 1 else parts[0]
        high = wide.astype(jnp.bfloat16)
        low = (wide - high.astype(jnp.float32)).astype(jnp.bfloat16)
        rows = jnp.dot(
            back_ref[...],
            jnp.concatenate([high, high, low], axis=0),
            preferred_element_type=jnp.float32,
        )
        for i in range(together):
            at = (first + i) * block
            convolved = rows[:, i * lanes : (i + 1) * lanes]
            begin = margin + at
            queries = taps_ref[0:1, :] * padded[begin : begin + block]
            for tap in range(1, taps_ref.shape[0] // 3):
                shifted = padded[begin - tap : begin - tap + block]
                queries = queries + taps_ref[tap : tap + 1, :] * shifted
            gated = queries * (convolved + skip_ref[...] * mixed[at : at + block])
            store_gated(out_ref, at, gated.astype(out_ref.dtype))


def complete_mixed(arrived_ref, taps_ref, mixed, edges):
    slabs = arrived_ref.shape[0]
    slab_rows = mixed.shape[0] // slabs
    taps = taps_ref.shape[0] // 3
    reach = taps - 1
    edges[:EDGE_ROWS] = jnp.zeros((EDGE_ROWS, edges.shape[1]), jnp.float32)
    for slab in range(slabs):
        at = (slab + 1) * EDGE_ROWS
        edges[at : at + EDGE_ROWS] = arrived_ref[slab, 3 * slab_rows :].astype(jnp.float32)

    def raw(kind, row):
        if row >= 0:
            return edges[pl.ds(EDGE_ROWS + kind * reach + row, slabs, stride=EDGE_ROWS), :]
        return edges[pl.ds((kind + 3) * reach + row, slabs, stride=EDGE_ROWS), :]

    for row in range(reach):
        product = None
        for kind in range(2):
            base = (kind + 1) * taps
            feature = taps_ref[base : base + 1, :] * raw(kind, row)
            for tap in range(1, taps):
                feature = feature + taps_ref[base + tap : base + tap + 1, :] * raw(kind, row - tap)
            product = feature if product is None else product * feature
        rounded = product.astype(jnp.bfloat16).astype(jnp.float32)
        mixed[pl.ds(row, slabs, stride=slab_rows), :] = rounded


def store_gated(out_ref, at, gated):
    copies, per_half, _, slab_rows, _ = out_ref.shape
    for begin in range(0, gated.shape[0], slab_rows):
        slab = (at + begin) // slab_rows
        for copy in range(copies):
            out_ref[copy, slab % per_half, slab // per_half] = gated[begin : begin + slab_rows]


def project_kernel(parts, own_ref, gated_ref, *refs):
    weight_refs, (near_ref, far_ref, rows) = iter(refs[:-3]), refs[-3:]
    sources, count, lanes = gated_ref.shape
    for source in range(sources):
        rows[:, source * lanes : (source + 1) * lanes] = gated_ref[source]
    swap = own_ref[0] == 1
    columns = near_ref.shape[1] // len(parts)
    for block, part_count in enumerate(parts):
        sums, begin = None, 0
        for weight_ref in itertools.islice(weight_refs, part_count):
            end = begin + weight_ref.shape[0]
            added = jnp.dot(rows[:, begin:end], weight_ref[...], preferred_element_type=jnp.float32)
            sums, begin = added if sums is None else sums + added, end
        first = sums[: count // 2].astype(near_ref.dtype)
        second = sums[count // 2 :].astype(near_ref.dtype)
        target = slice(block * columns, (block + 1) * columns)
        near_ref[:, target] = jnp.where(swap, second, first)
        far_ref[:, target] = jnp.where(swap, first, second)


def finish_kernel(first_offsets, place_ref, *refs):
    *pair_refs, out_ref = refs
    offset = 0
    for at, count in enumerate(first_offsets):
        near_ref, far_ref = pair_refs[2 * at : 2 * at + 2]
        columns = near_ref.shape[1] // count
        for block in range(count):
            source = slice(block * columns, (block + 1) * columns)
            total = near_ref[:, source].astype(jnp.float32) + far_ref[:, source].astype(jnp.float32)
            begin = (place_ref[0] ^ offset) * columns
            out_ref[:, pl.ds(pl.multiple_of(begin, columns), columns)] = total.astype(out_ref.dtype)
            offset += 1


def pack_kernel(qkv_ref, taps_ref, filter_ref, out_ref, padded, edges):
    targets, _, lanes = out_ref.shape
    rows = filter_ref.shape[0]
    reach = taps_ref.shape[1] - 1
    margin = padded.shape[0] - rows
    padded[:margin] = jnp.zeros((margin, padded.shape[1]), jnp.float32)
    edges[...] = jnp.zeros(edges.shape, jnp.float32)
    mixed_in = None
    for kind in (1, 2):
        padded[margin:] = qkv_ref[kind].astype(jnp.float32)
        feature = taps_ref[kind, 0:1] * padded[margin:]
        for tap in range(1, reach + 1):
            shifted = padded[margin - tap : margin - tap + rows]
            feature = feature + taps_ref[kind, tap : tap + 1] * shifted
        mixed_in = feature if mixed_in is None else mixed_in * feature
        edges[(kind - 1) * reach : kind * reach] = padded[margin : margin + reach]
        edges[(kind + 1) * reach : (kind + 2) * reach] = padded[margin + rows - reach :]
    for target in range(targets):
        at = slice(target * lanes, (target + 1) * lanes)
        out_ref[target, :rows] = filter_ref[:, at].astype(out_ref.dtype)
        out_ref[target, rows : 2 * rows] = qkv_ref[0, :, at]
        out_ref[target, 2 * rows : 3 * rows] = mixed_in[:, at].astype(out_ref.dtype)
        out_ref[target, 3 * rows :] = edges[:, at].astype(out_ref.dtype)


def pack(by_kind, short_taps, long_filter, peers):
    kinds, rows, channels = by_kind.shape
    reach = short_taps.shape[1] - 1
    lanes = channels // peers
    total = 3 * rows + EDGE_ROWS
    if lanes % 128:
        features = []
        for kind in (1, 2):
            extended = jnp.pad(by_kind[kind].astype(jnp.float32), ((reach, 0), (0, 0)))
            feature = short_taps[kind, 0] * extended[reach:]
            for tap in range(1, reach + 1):
                feature = feature + short_taps[kind, tap] * extended[reach - tap : reach - tap + rows]
            features.append(feature)
        mixed_in = (features[0] * features[1]).astype(jnp.bfloat16)
        first = by_kind[1:, :reach].reshape(2 * reach, channels)
        last = by_kind[1:, rows - reach :].reshape(2 * reach, channels)
        spare = jnp.zeros((EDGE_ROWS - 4 * reach, channels), jnp.bfloat16)
        parts = [long_filter.astype(jnp.bfloat16), by_kind[0], mixed_in, first, last, spare]
        return jnp.concatenate(parts).reshape(total, peers, lanes).transpose(1, 0, 2)
    steps = 2 if peers % 2 == 0 else 1
    width = channels // steps
    return pl.pallas_call(
        pack_kernel,
        out_shape=jax.ShapeDtypeStruct((peers, total, lanes), jnp.bfloat16),
        grid=(steps,),
        in_specs=[
            pl.BlockSpec((kinds, rows, width), lambda i: (0, 0, i)),
            pl.BlockSpec((kinds, reach + 1, width), lambda i: (0, 0, i)),
            pl.BlockSpec((rows, width), lambda i: (0, i)),
        ],
        out_specs=pl.BlockSpec((peers // steps, total, lanes), lambda i: (i, 0, 0)),
        scratch_shapes=[
            pltpu.VMEM((rows + 8, width), jnp.float32),
            pltpu.VMEM((EDGE_ROWS, width), jnp.float32),
        ],
        compiler_params=pltpu.CompilerParams(vmem_limit_bytes=60 * 2**20),
        cost_estimate=pl.CostEstimate(
            flops=16 * rows * channels, bytes_accessed=16 * rows * channels, transcendentals=0
        ),
        name="pack",
    )(by_kind, short_taps, long_filter)


def gated_conv(arrived, taps, skip, slab_rows, copies):
    slabs, _, lanes = arrived.shape
    tokens = slabs * slab_rows
    forward, backward = transform_tables(BLOCK)
    spectra = pltpu.VMEM((tokens // BLOCK, 2 * BLOCK, lanes), jnp.float32)
    return pl.pallas_call(
        conv_kernel,
        out_shape=jax.ShapeDtypeStruct(
            (copies, slabs // copies, copies, slab_rows, lanes), jnp.bfloat16
        ),
        scratch_shapes=[spectra] * 3
        + [
            pltpu.VMEM((tokens + 8, lanes), jnp.float32),
            pltpu.VMEM((tokens, lanes), jnp.float32),
            pltpu.VMEM(((slabs + 1) * EDGE_ROWS, lanes), jnp.float32),
        ],
        compiler_params=pltpu.CompilerParams(
            vmem_limit_bytes=(48 if tokens > 2048 else 20) * 2**20
        ),
        cost_estimate=pl.CostEstimate(
            flops=28 * BLOCK * tokens * lanes, bytes_accessed=20 * tokens * lanes, transcendentals=0
        ),
        name="gated_conv",
    )(jnp.asarray(forward), jnp.asarray(backward), arrived, taps, skip)


def project(own, gated, weights):
    sources, count, lanes = gated.shape
    depth, columns = sources * lanes, weights[0][0].shape[1]
    half = jax.ShapeDtypeStruct((count // 2, len(weights) * columns), jnp.bfloat16)
    whole = pl.BlockSpec(memory_space=pltpu.VMEM)
    flat = [part for parts in weights for part in parts]
    return pl.pallas_call(
        functools.partial(project_kernel, [len(parts) for parts in weights]),
        out_shape=(half, half),
        in_specs=[pl.BlockSpec(memory_space=pltpu.SMEM)] + [whole] * (1 + len(flat)),
        out_specs=(whole, whole),
        scratch_shapes=[pltpu.VMEM((count, depth), jnp.bfloat16)],
        compiler_params=pltpu.CompilerParams(vmem_limit_bytes=20 * 2**20),
        cost_estimate=pl.CostEstimate(
            flops=2 * count * depth * len(weights) * columns,
            bytes_accessed=2 * depth * len(weights) * columns + 4 * count * depth,
            transcendentals=0,
        ),
        name="project",
    )(own, gated, *flat)


def finish(place, pairs, blocks):
    rows = pairs[0][0].shape[0]
    columns = sum(near.shape[1] for near, _ in pairs)
    whole = pl.BlockSpec(memory_space=pltpu.VMEM)
    return pl.pallas_call(
        functools.partial(finish_kernel, blocks),
        out_shape=jax.ShapeDtypeStruct((rows, columns), jnp.bfloat16),
        in_specs=[pl.BlockSpec(memory_space=pltpu.SMEM)] + [whole] * (2 * len(pairs)),
        out_specs=whole,
        compiler_params=pltpu.CompilerParams(vmem_limit_bytes=20 * 2**20),
        cost_estimate=pl.CostEstimate(
            flops=rows * columns, bytes_accessed=6 * rows * columns, transcendentals=0
        ),
        name="finish",
    )(place, *[partial for pair in pairs for partial in pair])


def own_columns(array, lanes):
    return lax.dynamic_slice_in_dim(array, lax.axis_index("ctx") * lanes, lanes, axis=1)


def from_partner(value, offset):
    pairs = [(i, i ^ offset) for i in range(lax.axis_size("ctx"))]
    return lax.ppermute(value, "ctx", pairs)


def weights_on_the_way(out_weight):
    upper = out_weight[: out_weight.shape[0] // 2]
    return {0: [out_weight], 2: [from_partner(out_weight, 2)], 4: [from_partner(upper, 4)]}


def weights_passed_on(pieces, lower):
    return {**pieces, 4: pieces[4] + [from_partner(lower, 4)], 6: [from_partner(pieces[4][0], 2)]}


def weights_between_cores(pieces):
    pieces = {**pieces, 6: pieces[6] + [from_partner(pieces[4][1], 2)]}
    for at in (1, 3, 5, 7):
        pieces[at] = [from_partner(part, 1) for part in pieces[at ^ 1]]
    return [pieces[at] for at in range(8)]


def project_on_halves(gated, weights):
    half = lax.axis_size("ctx") // 2
    sources, halves, slab_rows, lanes = gated.shape
    rows = gated.reshape(sources, halves * slab_rows, lanes)
    own = lax.axis_index("tp").astype(jnp.int32)[None]
    place = (lax.axis_index("ctx") % half).astype(jnp.int32)[None]
    blocks = [len(weights) // 2] * 2
    arrived = []
    for part in (weights[: blocks[0]], weights[blocks[0] :]):
        partials = project(own, rows, part)
        arrived.append([to_their_place(partial, other) for other, partial in enumerate(partials)])
    return finish(place, arrived, blocks)


def to_their_place(partial, other):
    half = lax.axis_size("ctx") // 2
    pairs = []
    for side in range(2):
        for slab in range(half):
            for own in range(2):
                source = (side * half + slab) * 2 + own
                target = ((own ^ other) * half + slab) * 2 + side
                pairs.append((source, target))
    return lax.ppermute(partial, ("ctx", "tp"), pairs)


def project_whole(gated, out_weight):
    sources, _, slab_rows, lanes = gated.shape
    rows = gated.reshape(sources, slab_rows, lanes).transpose(1, 0, 2)
    partials = jnp.dot(
        rows.reshape(slab_rows, sources * lanes),
        lax.all_gather(out_weight, "ctx", axis=1, tiled=True),
        preferred_element_type=jnp.float32,
    )
    return lax.psum_scatter(partials, "tp", scatter_dimension=1, tiled=True).astype(jnp.bfloat16)


def body(qkv_in, short_taps, long_filter, skip_gain, out_weight):
    channel_count = qkv_in.shape[2]
    peers = lax.axis_size("ctx")
    lanes = channel_count // peers
    copies = 2 if lax.axis_size("tp") == 2 and peers == 16 else 1

    packed = pack(qkv_in.transpose(1, 0, 2), short_taps, long_filter, peers)
    arrived = lax.all_to_all(packed, "ctx", split_axis=0, concat_axis=0, tiled=True)
    if copies == 2:
        own_weight, _ = lax.optimization_barrier((out_weight, packed))
        pieces = weights_on_the_way(own_weight)
        lower = own_weight[own_weight.shape[0] // 2 :]
        (pieces, lower), _ = lax.optimization_barrier(((pieces, lower), arrived))
        pieces = weights_passed_on(pieces, lower)

    taps = own_columns(short_taps.reshape(-1, channel_count), lanes)
    skip = own_columns(skip_gain[None, :], lanes)
    gated = gated_conv(arrived, taps, skip, qkv_in.shape[0], copies)
    if copies == 2:
        gated, pieces = lax.optimization_barrier((gated, pieces))
        weights = weights_between_cores(pieces)
    by_target = gated.reshape(peers, copies, *gated.shape[3:])
    landed = lax.all_to_all(by_target, "ctx", split_axis=0, concat_axis=0, tiled=True)
    if copies == 2:
        return project_on_halves(landed, weights)
    return project_whole(landed, out_weight)


def solution(mesh):
    return jax.shard_map(
        body,
        mesh=mesh,
        in_specs=(
            P("ctx", None, "tp"),
            P(None, None, "tp"),
            P("ctx", "tp"),
            P("tp"),
            P("tp", "ctx"),
        ),
        out_specs=P("ctx", "tp"),
        check_vma=False,
    )
```

time: 613 us -> 134 us (0.22); the launches traced: 605 us -> 133 us
  waiting for transfers between devices: 312 us -> 82.3 us
  matrix products: 81.1 us -> 0 us
  starting transfers between devices: 106 us -> 27.5 us
  local copies, waits for them, and re-layouts: 45.2 us -> 5.51 us
  blocking collectives: 35.9 us -> 0 us
  Pallas kernels: 0 us -> 17.6 us
  between operations: 14 us -> 0.16 us
  other arithmetic: 11.2 us -> 0 us
    all_to_all x8 -> x2, waiting for transfers between devices: 281 us -> 0.01 us  [the longest x1 0.01 us: body(): lax.all_to_all(packed, 'ctx', split_axis=0, concat_axis=0, tiled=True)]
    all_to_all x8 -> x2, starting transfers between devices: 101 us -> 12.8 us  [the longest x1 6.62 us: body(): lax.all_to_all(packed, 'ctx', split_axis=0, concat_axis=0, tiled=True)]
    ppermute x1 -> x15, waiting for transfers between devices: 0.01 us -> 82.3 us  [the longest x11 64.6 us: from_partner(): return lax.ppermute(value, 'ctx', pairs)]
    dot_general x19 -> x0, matrix products: 81.1 us -> none  [the longest x12 55.8 us: contract(): return jnp.einsum('ki,aic->akc', matrix, operand, precision=highest)]
    all_to_all x1 -> x0, blocking collectives: 35.9 us -> none  [over_slabs(): lax.all_to_all(output.reshape(peer_count, block_rows, channel_count), 'ct...]
    reduce_scatter x1 -> x0, waiting for transfers between devices: 30.3 us -> none  [body(): lax.psum_scatter(partials, 'tp', scatter_dimension=1, tiled=True)]
    pallas_call x0 -> x5, Pallas kernels: none -> 17.6 us  [the longest x2 6.53 us: project(): pl.pallas_call(functools.partial(project_kernel, [len(parts) for parts in...]
    add x3 -> x0, local copies, waits for them, and re-layouts: 12.5 us -> none  [the longest x2 8.23 us: rotate(): real_part * sin_table + imag_part * cos_table]
  transfers between devices with their start and end apart: 11 -> 17, of which waited for: 9 -> 7; matrix products, arithmetic and copies ran while one was open for 20% -> 1% of each run, Pallas kernels for 0% -> 10%
where the time goes in v1:
time: 134 us; the launch traced here: 133 us
  waiting for transfers between devices  82.3 us (61%)
  starting transfers between devices  27.5 us (21%)
  Pallas kernels  17.6 us (13%)
  local copies, waits for them, and re-layouts  5.51 us (4%)
    ppermute x11, waiting for transfers between devices, from_partner(): return lax.ppermute(value, 'ctx', pairs)  64.6 us
    ppermute x4, waiting for transfers between devices, to_their_place(): return lax.ppermute(partial, ('ctx', 'tp'), pairs)  17.6 us
    ppermute x11, starting transfers between devices, from_partner(): return lax.ppermute(value, 'ctx', pairs)  7.52 us
    ppermute x4, starting transfers between devices, to_their_place(): return lax.ppermute(partial, ('ctx', 'tp'), pairs)  7.18 us
    all_to_all x1, starting transfers between devices, body(): lax.all_to_all(packed, 'ctx', split_axis=0, concat_axis=0, tiled=True)  6.62 us
    pallas_call x2, Pallas kernels, project(): pl.pallas_call(functools.partial(project_kernel, [len(parts) for parts in...  6.53 us
    pallas_call x1, Pallas kernels, gated_conv(): pl.pallas_call(conv_kernel, out_shape=jax.ShapeDtypeStruct((copies, slabs...  6.43 us
    all_to_all x1, starting transfers between devices, body(): lax.all_to_all(by_target, 'ctx', split_axis=0, concat_axis=0, tiled=True)  6.22 us
  transfers between devices with their start and end apart: 17, of which 7 were waited for; matrix products, arithmetic and copies ran while one was open for 1% of the time, Pallas kernels for 10%

profile of v1, /device:TPU:5, one launch (start us, length us, event | category | flops | bytes accessed | tf_op | source)
XLA Modules:
  0.0 133.1 jit_solution(17810327082061889427)
XLA Ops:
  0.0 0.0 copy-start
  0.0 3.7 %pack.1 = bf16[16,400,128]{2,1,0:T(8,128)(2,1)} custom-call(bf16[3,128,2048]{2,1,0:T(8,128)(2,1)} %bitcast.9, f32[3,3,2048]{2,1,0:T(4,128)} %taps_ref.1, f32[128,2048]{1,0:T(8,128)} %filter_ref.1), custom_call_target="tpu_custom_call" | custom-call | flops 4194304 | bytes 4194304 | tf_op jit(solution)/shard_map/pack/pallas_call | solution.py:286
  3.7 0.0 copy-start.1
  3.7 6.6 %all-to-all-start = ((bf16[16,400,128]{2,1,0:T(8,128)(2,1)}), bf16[16,400,128]{2,1,0:T(8,128)(2,1)}, u32[]{:S(2)}, u32[]{:S(2)}) async-start(bf16[16,400,128]{2,1,0:T(8,128)(2,1)} %pack.1), calls=%async_computation | async-start | bytes 3276800 | tf_op jit(solution)/shard_map/all_to_all | solution.py:442
  10.4 0.0 copy-done.1
  10.4 0.0 copy-start.10
  10.4 1.5 %collective-permute-start = (bf16[2048,256]{1,0:T(8,128)(2,1)S(1)}, bf16[2048,256]{1,0:T(8,128)(2,1)S(1)}, u32[]{:S(2)}, u32[]{:S(2)}) collective-permute-start(bf16[2048,256]{1,0:T(8,128)(2,1)S(1)} %copy-done.1), channel_id=1, source_target_pairs={{0,4},{2,6},{4,0},{6,2},{8,12},{10,14},{12,8},{14,10},{16,20},{18,... | collective-permute-start | bytes 3145736 | tf_op jit(solution)/shard_map/ppermute | solution.py:379
  11.8 0.9 fusion
  12.7 1.2 collective-permute-start.1
  13.9 36.4 %collective-permute-done.1.refs_0_ = bf16[1024,256]{1,0:T(8,128)(2,1)S(1)} collective-permute-done((bf16[1024,256]{1,0:T(8,128)(2,1)S(1)}, bf16[1024,256]{1,0:T(8,128)(2,1)S(1)}, u32[]{:S(2)}, u32[]{:S(2)}) %collective-permute-start.1) | collective-permute-done | bytes 524320 | tf_op jit(solution)/shard_map/ppermute | solution.py:379
  50.3 0.0 copy-start.4
  50.3 2.4 %collective-permute-done.refs_2_ = bf16[2048,256]{1,0:T(8,128)(2,1)S(1)} collective-permute-done((bf16[2048,256]{1,0:T(8,128)(2,1)S(1)}, bf16[2048,256]{1,0:T(8,128)(2,1)S(1)}, u32[]{:S(2)}, u32[]{:S(2)}) %collective-permute-start) | collective-permute-done | bytes 1048608 | tf_op jit(solution)/shard_map/ppermute | solution.py:379
  52.8 0.0 all-to-all-done.arrived_ref
  52.8 1.2 collective-permute-start.2
  53.9 0.3 collective-permute-start.3
  54.2 0.0 copy-done.10
  54.3 0.0 copy-done
  54.3 0.1 dynamic-slice_bitcast_fusion.skip_ref
  54.4 0.0 copy-start.8
  54.4 1.1 copy-done.8
  55.5 0.0 copy-start.9
  55.5 1.0 copy-done.9
  56.5 6.4 %gated_conv.1 = bf16[2,8,2,128,128]{4,3,2,1,0:T(8,128)(2,1)} custom-call(bf16[512,512]{1,0:T(8,128)(2,1)S(1)} %copy-done.9, bf16[256,1536]{1,0:T(8,128)(2,1)S(1)} %copy-done.8, bf16[16,400,128]{2,1,0:T(8,128)(2,1)} %all-to-all-done.arrived_ref, f32[9,128]{1,0:T(8,128)S(1)} %constant_dynamic-slice_fusion.taps_ref, f32[1,128]{1,0:T(1,128)S(1)} %dynamic-slice_bitcast_fusion.skip_ref), custom_call_target="tpu_custom_call" | custom-call | flops 1879048192 | bytes 5242880 | tf_op jit(solution)/shard_map/gated_conv/pallas_call | solution.py:313
  63.0 0.0 copy-done.4
  63.0 2.7 %collective-permute-done.2.refs_1_ = bf16[1024,256]{1,0:T(8,128)(2,1)S(1)} collective-permute-done((bf16[1024,256]{1,0:T(8,128)(2,1)}, bf16[1024,256]{1,0:T(8,128)(2,1)S(1)}, u32[]{:S(2)}, u32[]{:S(2)}) %collective-permute-start.2) | collective-permute-done | bytes 524320 | tf_op jit(solution)/shard_map/ppermute | solution.py:379
  65.6 0.0 copy-start.6
  65.6 0.7 collective-permute-done.3.refs_4_
  66.3 0.1 copy-done.6
  66.4 6.2 %all-to-all-start.1 = ((bf16[16,2,128,128]{3,2,1,0:T(8,128)(2,1)}), bf16[16,2,128,128]{3,2,1,0:T(8,128)(2,1)S(1)}, u32[]{:S(2)}, u32[]{:S(2)}) async-start(bf16[16,2,128,128]{3,2,1,0:T(8,128)(2,1)} %bitcast.4), calls=%async_computation.1 | async-start | bytes 2097152 | tf_op jit(solution)/shard_map/all_to_all | solution.py:457
  72.7 0.2 collective-permute-start.4
  72.8 0.3 collective-permute-start.5
  73.2 1.4 %collective-permute-start.10 = (bf16[1024,256]{1,0:T(8,128)(2,1)}, bf16[1024,256]{1,0:T(8,128)(2,1)}, u32[]{:S(2)}, u32[]{:S(2)}) collective-permute-start(bf16[1024,256]{1,0:T(8,128)(2,1)} %copy-done.6), channel_id=1, source_target_pairs={{0,4},{2,6},{4,0},{6,2},{8,12},{10,14},{12,8},{14,10},{16,20},{18,... | collective-permute-start | bytes 1572872 | tf_op jit(solution)/shard_map/ppermute | solution.py:379
  74.6 0.6 collective-permute-start.9
  75.2 0.0 collective-permute-start.8
  75.2 22.4 %collective-permute-done.10.refs_5_ = bf16[1024,256]{1,0:T(8,128)(2,1)} collective-permute-done((bf16[1024,256]{1,0:T(8,128)(2,1)}, bf16[1024,256]{1,0:T(8,128)(2,1)}, u32[]{:S(2)}, u32[]{:S(2)}) %collective-permute-start.10) | collective-permute-done | bytes 524320 | tf_op jit(solution)/shard_map/ppermute | solution.py:379
  97.6 0.9 collective-permute-start.11
  98.5 0.0 collective-permute-done.4.refs_1_
  98.5 0.0 copy-start.2
  98.5 1.0 copy-done.2
  99.5 0.0 collective-permute-start.12
  99.5 0.0 collective-permute-done.5.refs_3_
  99.5 0.0 all-to-all-done.1
  99.5 0.0 copy-start.3
  99.5 1.2 copy-done.3
  100.7 0.0 copy-start.5
  100.7 0.0 copy-start.7
  100.7 3.4 %project.2 = (bf16[128,1024]{1,0:T(8,128)(2,1)}, bf16[128,1024]{1,0:T(8,128)(2,1)S(1)}) custom-call(s32[1]{0:T(128)} %bitcast.1.own_ref, bf16[16,256,128]{2,1,0:T(8,128)(2,1)S(1)} %bitcast.7, bf16[2048,256]{1,0:T(8,128)(2,1)S(1)} %copy-done.1, bf16[2048,256]{1,0:T(8,128)(2,1)S(1)} %copy-done.3, bf16[2048,256]{1,0:T(8,128)(2,1)S(1)} %collective-permute-done.refs_2_, ...), custom_call_target="tpu_custom_call" | custom-call | flops 1073741824 | bytes 6291456 | tf_op jit(solution)/shard_map/project/pallas_call | solution.py:340
  104.1 2.9 %collective-permute-start.6 = (bf16[128,1024]{1,0:T(8,128)(2,1)}, bf16[128,1024]{1,0:T(8,128)(2,1)S(1)}, u32[]{:S(2)}, u32[]{:S(2)}) collective-permute-start(bf16[128,1024]{1,0:T(8,128)(2,1)} %get-tuple-element.28), channel_id=1, source_target_pairs={{0,0},{1,16},{2,2},{3,18},{4,4},{5,20},{6,6},{7,22},{8,8},{9,24},{... | collective-permute-start | bytes 786440 | tf_op jit(solution)/shard_map/ppermute | solution.py:421
  107.0 0.0 collective-permute-done.8.refs_2_
  107.0 0.1 collective-permute-start.7
  107.1 0.0 collective-permute-done.9.refs_3_
  107.1 0.0 collective-permute-done.11.refs_6_
  107.1 0.0 collective-permute-done.12.refs_7_
  107.1 0.0 copy-done.5
  107.1 0.0 copy-done.7
  107.1 3.2 %project.3 = (bf16[128,1024]{1,0:T(8,128)(2,1)S(1)}, bf16[128,1024]{1,0:T(8,128)(2,1)S(1)}) custom-call(s32[1]{0:T(128)} %bitcast.1.own_ref, bf16[16,256,128]{2,1,0:T(8,128)(2,1)S(1)} %bitcast.8, bf16[1024,256]{1,0:T(8,128)(2,1)S(1)} %copy-done.5, bf16[1024,256]{1,0:T(8,128)(2,1)S(1)} %copy-done.7, bf16[1024,256]{1,0:T(8,128)(2,1)} %collective-permute-done.8.refs_2_, ...), custom_call_target="tpu_custom_call" | custom-call | flops 1073741824 | bytes 6291456 | tf_op jit(solution)/shard_map/project/pallas_call | solution.py:340
  110.3 4.1 %collective-permute-start.13 = (bf16[128,1024]{1,0:T(8,128)(2,1)S(1)}, bf16[128,1024]{1,0:T(8,128)(2,1)S(1)}, u32[]{:S(2)}, u32[]{:S(2)}) collective-permute-start(bf16[128,1024]{1,0:T(8,128)(2,1)S(1)} %get-tuple-element.33), channel_id=1, source_target_pairs={{0,0},{1,16},{2,2},{3,18},{4,4},{5,20},{6,6},{7,22},{8,8},{9,24},{... | collective-permute-start | bytes 786440 | tf_op jit(solution)/shard_map/ppermute | solution.py:421
  114.5 0.1 collective-permute-start.14
  114.5 12.0 %collective-permute-done.6.refs_0_ = bf16[128,1024]{1,0:T(8,128)(2,1)S(1)} collective-permute-done((bf16[128,1024]{1,0:T(8,128)(2,1)}, bf16[128,1024]{1,0:T(8,128)(2,1)S(1)}, u32[]{:S(2)}, u32[]{:S(2)}) %collective-permute-start.6) | collective-permute-done | bytes 262176 | tf_op jit(solution)/shard_map/ppermute | solution.py:421
  126.6 0.0 collective-permute-done.7.refs_1_
  126.6 5.6 %collective-permute-done.13.refs_2_ = bf16[128,1024]{1,0:T(8,128)(2,1)S(1)} collective-permute-done((bf16[128,1024]{1,0:T(8,128)(2,1)S(1)}, bf16[128,1024]{1,0:T(8,128)(2,1)S(1)}, u32[]{:S(2)}, u32[]{:S(2)}) %collective-permute-start.13) | collective-permute-done | bytes 262176 | tf_op jit(solution)/shard_map/ppermute | solution.py:421
  132.2 0.0 collective-permute-done.14.refs_3_
  132.2 0.9 finish.1
  (2 shorter events, 0.0 us)
Async XLA Ops:
  0.0 54.3 %copy-start = (f32[2048]{0:T(1024)S(1)}, f32[2048]{0:T(1024)}, u32[]{:S(2)}) copy-start(f32[2048]{0:T(1024)} %param.10) | copy-start | bytes 24580
  3.7 6.6 %copy-start.1 = (bf16[2048,256]{1,0:T(8,128)(2,1)S(1)}, bf16[2048,256]{1,0:T(8,128)(2,1)}, u32[]{:S(2)}) copy-start(bf16[2048,256]{1,0:T(8,128)(2,1)} %refs_0_) | copy-start | bytes 3145732
  3.7 49.0 %all-to-all-start = ((bf16[16,400,128]{2,1,0:T(8,128)(2,1)}), bf16[16,400,128]{2,1,0:T(8,128)(2,1)}, u32[]{:S(2)}, u32[]{:S(2)}) async-start(bf16[16,400,128]{2,1,0:T(8,128)(2,1)} %pack.1), calls=%async_computation | async-start | bytes 3276800 | tf_op jit(solution)/shard_map/all_to_all | solution.py:442
  10.4 43.9 %copy-start.10 = (f32[3,3,2048]{2,1,0:T(4,128)S(1)}, f32[3,3,2048]{2,1,0:T(4,128)}, u32[]{:S(2)}) copy-start(f32[3,3,2048]{2,1,0:T(4,128)} %taps_ref.1) | copy-start | bytes 221188
  10.4 42.4 %collective-permute-start = (bf16[2048,256]{1,0:T(8,128)(2,1)S(1)}, bf16[2048,256]{1,0:T(8,128)(2,1)S(1)}, u32[]{:S(2)}, u32[]{:S(2)}) collective-permute-start(bf16[2048,256]{1,0:T(8,128)(2,1)S(1)} %copy-done.1), channel_id=1, source_target_pairs={{0,4},{2,6},{4,0},{6,2},{8,12},{10,14},{12,8},{14,10},{16,20},{18,... | collective-permute-start | bytes 3145736 | tf_op jit(solution)/shard_map/ppermute | solution.py:379
  12.7 37.6 %collective-permute-start.1 = (bf16[1024,256]{1,0:T(8,128)(2,1)S(1)}, bf16[1024,256]{1,0:T(8,128)(2,1)S(1)}, u32[]{:S(2)}, u32[]{:S(2)}) collective-permute-start(bf16[1024,256]{1,0:T(8,128)(2,1)S(1)} %get-tuple-element.36), channel_id=1, source_target_pairs={{0,8},{2,10},{4,12},{6,14},{8,0},{10,2},{12,4},{14,6},{16,24},{18,... | collective-permute-start | bytes 1572872 | tf_op jit(solution)/shard_map/ppermute | solution.py:379
  50.3 12.6 %copy-start.4 = (bf16[1024,256]{1,0:T(8,128)(2,1)}, bf16[1024,256]{1,0:T(8,128)(2,1)S(1)}, u32[]{:S(2)}) copy-start(bf16[1024,256]{1,0:T(8,128)(2,1)S(1)} %collective-permute-done.1.refs_0_) | copy-start | bytes 1572868
  52.8 12.9 %collective-permute-start.2 = (bf16[1024,256]{1,0:T(8,128)(2,1)}, bf16[1024,256]{1,0:T(8,128)(2,1)S(1)}, u32[]{:S(2)}, u32[]{:S(2)}) collective-permute-start(bf16[1024,256]{1,0:T(8,128)(2,1)} %get-tuple-element.24), channel_id=1, source_target_pairs={{0,8},{2,10},{4,12},{6,14},{8,0},{10,2},{12,4},{14,6},{16,24},{18,... | collective-permute-start | bytes 1572872 | tf_op jit(solution)/shard_map/ppermute | solution.py:379
  53.9 12.4 %collective-permute-start.3 = (bf16[1024,256]{1,0:T(8,128)(2,1)S(1)}, bf16[1024,256]{1,0:T(8,128)(2,1)}, u32[]{:S(2)}, u32[]{:S(2)}) collective-permute-start(bf16[1024,256]{1,0:T(8,128)(2,1)S(1)} %collective-permute-done.1.refs_0_), channel_id=1, source_target_pairs={{0,4},{2,6},{4,0},{6,2},{8,12},{10,14},{12,8},{14,10},{16,20},{18,... | collective-permute-start | bytes 1572872 | tf_op jit(solution)/shard_map/ppermute | solution.py:379
  54.4 1.1 copy-start.8
  55.5 1.0 copy-start.9
  65.6 0.8 copy-start.6
  66.4 33.0 %all-to-all-start.1 = ((bf16[16,2,128,128]{3,2,1,0:T(8,128)(2,1)}), bf16[16,2,128,128]{3,2,1,0:T(8,128)(2,1)S(1)}, u32[]{:S(2)}, u32[]{:S(2)}) async-start(bf16[16,2,128,128]{3,2,1,0:T(8,128)(2,1)} %bitcast.4), calls=%async_computation.1 | async-start | bytes 2097152 | tf_op jit(solution)/shard_map/all_to_all | solution.py:457
  72.7 25.8 %collective-permute-start.4 = (bf16[2048,256]{1,0:T(8,128)(2,1)S(1)}, bf16[2048,256]{1,0:T(8,128)(2,1)S(1)}, u32[]{:S(2)}, u32[]{:S(2)}) collective-permute-start(bf16[2048,256]{1,0:T(8,128)(2,1)S(1)} %copy-done.1), channel_id=1, source_target_pairs={{0,2},{2,0},{4,6},{6,4},{8,10},{10,8},{12,14},{14,12},{16,18},{18,... | collective-permute-start | bytes 3145736 | tf_op jit(solution)/shard_map/ppermute | solution.py:379
  72.8 26.6 %collective-permute-start.5 = (bf16[2048,256]{1,0:T(8,128)(2,1)S(1)}, bf16[2048,256]{1,0:T(8,128)(2,1)}, u32[]{:S(2)}, u32[]{:S(2)}) collective-permute-start(bf16[2048,256]{1,0:T(8,128)(2,1)S(1)} %collective-permute-done.refs_2_), channel_id=1, source_target_pairs={{0,2},{2,0},{4,6},{6,4},{8,10},{10,8},{12,14},{14,12},{16,18},{18,... | collective-permute-start | bytes 3145736 | tf_op jit(solution)/shard_map/ppermute | solution.py:379
  73.2 24.4 %collective-permute-start.10 = (bf16[1024,256]{1,0:T(8,128)(2,1)}, bf16[1024,256]{1,0:T(8,128)(2,1)}, u32[]{:S(2)}, u32[]{:S(2)}) collective-permute-start(bf16[1024,256]{1,0:T(8,128)(2,1)} %copy-done.6), channel_id=1, source_target_pairs={{0,4},{2,6},{4,0},{6,2},{8,12},{10,14},{12,8},{14,10},{16,20},{18,... | collective-permute-start | bytes 1572872 | tf_op jit(solution)/shard_map/ppermute | solution.py:379
  74.6 32.5 %collective-permute-start.9 = (bf16[1024,256]{1,0:T(8,128)(2,1)}, bf16[1024,256]{1,0:T(8,128)(2,1)}, u32[]{:S(2)}, u32[]{:S(2)}) collective-permute-start(bf16[1024,256]{1,0:T(8,128)(2,1)} %copy-done.6), channel_id=1, source_target_pairs={{0,2},{2,0},{4,6},{6,4},{8,10},{10,8},{12,14},{14,12},{16,18},{18,... | collective-permute-start | bytes 1572872 | tf_op jit(solution)/shard_map/ppermute | solution.py:379
  75.2 31.8 %collective-permute-start.8 = (bf16[1024,256]{1,0:T(8,128)(2,1)}, bf16[1024,256]{1,0:T(8,128)(2,1)}, u32[]{:S(2)}, u32[]{:S(2)}) collective-permute-start(bf16[1024,256]{1,0:T(8,128)(2,1)} %copy-done.4), channel_id=1, source_target_pairs={{0,2},{2,0},{4,6},{6,4},{8,10},{10,8},{12,14},{14,12},{16,18},{18,... | collective-permute-start | bytes 1572872 | tf_op jit(solution)/shard_map/ppermute | solution.py:379
  97.6 9.5 %collective-permute-start.11 = (bf16[1024,256]{1,0:T(8,128)(2,1)}, bf16[1024,256]{1,0:T(8,128)(2,1)}, u32[]{:S(2)}, u32[]{:S(2)}) collective-permute-start(bf16[1024,256]{1,0:T(8,128)(2,1)} %collective-permute-done.3.refs_4_), channel_id=1, source_target_pairs={{0,2},{2,0},{4,6},{6,4},{8,10},{10,8},{12,14},{14,12},{16,18},{18,... | collective-permute-start | bytes 1572872 | tf_op jit(solution)/shard_map/ppermute | solution.py:379
  98.5 1.0 copy-start.2
  99.5 7.7 %collective-permute-start.12 = (bf16[1024,256]{1,0:T(8,128)(2,1)}, bf16[1024,256]{1,0:T(8,128)(2,1)}, u32[]{:S(2)}, u32[]{:S(2)}) collective-permute-start(bf16[1024,256]{1,0:T(8,128)(2,1)} %collective-permute-done.10.refs_5_), channel_id=1, source_target_pairs={{0,2},{2,0},{4,6},{6,4},{8,10},{10,8},{12,14},{14,12},{16,18},{18,... | collective-permute-start | bytes 1572872 | tf_op jit(solution)/shard_map/ppermute | solution.py:379
  99.5 1.2 copy-start.3
  100.7 6.4 %copy-start.5 = (bf16[1024,256]{1,0:T(8,128)(2,1)S(1)}, bf16[1024,256]{1,0:T(8,128)(2,1)}, u32[]{:S(2)}) copy-start(bf16[1024,256]{1,0:T(8,128)(2,1)} %copy-done.4) | copy-start | bytes 1572868
  100.7 6.4 %copy-start.7 = (bf16[1024,256]{1,0:T(8,128)(2,1)S(1)}, bf16[1024,256]{1,0:T(8,128)(2,1)}, u32[]{:S(2)}) copy-start(bf16[1024,256]{1,0:T(8,128)(2,1)} %copy-done.6) | copy-start | bytes 1572868
  104.1 22.5 %collective-permute-start.6 = (bf16[128,1024]{1,0:T(8,128)(2,1)}, bf16[128,1024]{1,0:T(8,128)(2,1)S(1)}, u32[]{:S(2)}, u32[]{:S(2)}) collective-permute-start(bf16[128,1024]{1,0:T(8,128)(2,1)} %get-tuple-element.28), channel_id=1, source_target_pairs={{0,0},{1,16},{2,2},{3,18},{4,4},{5,20},{6,6},{7,22},{8,8},{9,24},{... | collective-permute-start | bytes 786440 | tf_op jit(solution)/shard_map/ppermute | solution.py:421
  107.0 19.5 %collective-permute-start.7 = (bf16[128,1024]{1,0:T(8,128)(2,1)S(1)}, bf16[128,1024]{1,0:T(8,128)(2,1)S(1)}, u32[]{:S(2)}, u32[]{:S(2)}) collective-permute-start(bf16[128,1024]{1,0:T(8,128)(2,1)S(1)} %get-tuple-element.29), channel_id=1, source_target_pairs={{0,16},{1,0},{2,18},{3,2},{4,20},{5,4},{6,22},{7,6},{8,24},{9,8},{... | collective-permute-start | bytes 786440 | tf_op jit(solution)/shard_map/ppermute | solution.py:421
  110.3 21.9 %collective-permute-start.13 = (bf16[128,1024]{1,0:T(8,128)(2,1)S(1)}, bf16[128,1024]{1,0:T(8,128)(2,1)S(1)}, u32[]{:S(2)}, u32[]{:S(2)}) collective-permute-start(bf16[128,1024]{1,0:T(8,128)(2,1)S(1)} %get-tuple-element.33), channel_id=1, source_target_pairs={{0,0},{1,16},{2,2},{3,18},{4,4},{5,20},{6,6},{7,22},{8,8},{9,24},{... | collective-permute-start | bytes 786440 | tf_op jit(solution)/shard_map/ppermute | solution.py:421
  114.5 17.7 %collective-permute-start.14 = (bf16[128,1024]{1,0:T(8,128)(2,1)S(1)}, bf16[128,1024]{1,0:T(8,128)(2,1)S(1)}, u32[]{:S(2)}, u32[]{:S(2)}) collective-permute-start(bf16[128,1024]{1,0:T(8,128)(2,1)S(1)} %get-tuple-element.34), channel_id=1, source_target_pairs={{0,16},{1,0},{2,18},{3,2},{4,20},{5,4},{6,22},{7,6},{8,24},{9,8},{... | collective-permute-start | bytes 786440 | tf_op jit(solution)/shard_map/ppermute | solution.py:421

commit v2 on v1

--- a/solution.py
+++ b/solution.py
@@ -390,8 +390,9 @@
 
 def weights_between_cores(pieces):
     pieces = {**pieces, 6: pieces[6] + [from_partner(pieces[4][1], 2)]}
-    for at in (1, 3, 5, 7):
+    for at in (1, 3, 5):
         pieces[at] = [from_partner(part, 1) for part in pieces[at ^ 1]]
+    pieces[7] = [from_partner(pieces[6][0], 1)]
     return [pieces[at] for at in range(8)]
 
 
@@ -401,12 +402,16 @@
     rows = gated.reshape(sources, halves * slab_rows, lanes)
     own = lax.axis_index("tp").astype(jnp.int32)[None]
     place = (lax.axis_index("ctx") % half).astype(jnp.int32)[None]
-    blocks = [len(weights) // 2] * 2
-    arrived = []
-    for part in (weights[: blocks[0]], weights[blocks[0] :]):
-        partials = project(own, rows, part)
-        arrived.append([to_their_place(partial, other) for other, partial in enumerate(partials)])
-    return finish(place, arrived, blocks)
+    split = len(weights) // 2
+    first = project(own, rows, weights[:split])
+    last_part, _ = lax.optimization_barrier((weights[6][-1], first[0]))
+    weights[7] = weights[7] + [from_partner(last_part, 1)]
+    second = project(own, rows, weights[split:])
+    arrived = [
+        [to_their_place(partial, other) for other, partial in enumerate(partials)]
+        for partials in (first, second)
+    ]
+    return finish(place, arrived, [split, len(weights) - split])
 
 
 def to_their_place(partial, other):

time: 134 us -> 132 us (0.985)
  local copies, waits for them, and re-layouts: 5.51 us -> 3.3 us
  starting transfers between devices: 27.5 us -> 29.1 us
    ppermute x11, waiting for transfers between devices: 64.6 us -> 43.7 us  [from_partner(): return lax.ppermute(value, 'ctx', pairs)]
    all_to_all x1, waiting for transfers between devices: 0.01 us -> 18.9 us  [body(): lax.all_to_all(by_target, 'ctx', split_axis=0, concat_axis=0, tiled=True)]
    unnamed x22 -> x18, local copies, waits for them, and re-layouts: 4.53 us -> 2.32 us
    ppermute x4, starting transfers between devices: 7.18 us -> 9.38 us  [to_their_place(): return lax.ppermute(partial, ('ctx', 'tp'), pairs)]
  transfers between devices with their start and end apart: 17 -> 17, of which waited for: 7 -> 11; matrix products, arithmetic and copies ran while one was open for 1% -> 1% of each run, Pallas kernels for 10% -> 10%
where the time goes in v2:
time: 132 us; the launch traced here: 131 us
  waiting for transfers between devices  81.1 us (61%)
  starting transfers between devices  29.1 us (22%)
  Pallas kernels  17.8 us (13%)
  local copies, waits for them, and re-layouts  3.3 us (2%)
    ppermute x11, waiting for transfers between devices, from_partner(): return lax.ppermute(value, 'ctx', pairs)  43.7 us
    all_to_all x1, waiting for transfers between devices, body(): lax.all_to_all(by_target, 'ctx', split_axis=0, concat_axis=0, tiled=True)  18.9 us
    ppermute x4, waiting for transfers between devices, to_their_place(): return lax.ppermute(partial, ('ctx', 'tp'), pairs)  18.5 us
    ppermute x4, starting transfers between devices, to_their_place(): return lax.ppermute(partial, ('ctx', 'tp'), pairs)  9.38 us
    ppermute x11, starting transfers between devices, from_partner(): return lax.ppermute(value, 'ctx', pairs)  6.91 us
    pallas_call x2, Pallas kernels, project(): pl.pallas_call(functools.partial(project_kernel, [len(parts) for parts in...  6.75 us
    all_to_all x1, starting transfers between devices, body(): lax.all_to_all(packed, 'ctx', split_axis=0, concat_axis=0, tiled=True)  6.62 us
    pallas_call x1, Pallas kernels, gated_conv(): pl.pallas_call(conv_kernel, out_shape=jax.ShapeDtypeStruct((copies, slabs...  6.42 us
  transfers between devices with their start and end apart: 17, of which 11 were waited for; matrix products, arithmetic and copies ran while one was open for 1% of the time, Pallas kernels for 10%

profile of v2, /device:TPU:5, one launch (start us, length us, event | category | flops | bytes accessed | tf_op | source)
XLA Modules:
  0.0 131.4 jit_solution(4160670572610862872)
XLA Ops:
  0.0 0.0 copy-start
  0.0 3.7 %pack.1 = bf16[16,400,128]{2,1,0:T(8,128)(2,1)} custom-call(bf16[3,128,2048]{2,1,0:T(8,128)(2,1)} %bitcast.9, f32[3,3,2048]{2,1,0:T(4,128)} %taps_ref.1, f32[128,2048]{1,0:T(8,128)} %filter_ref.1), custom_call_target="tpu_custom_call" | custom-call | flops 4194304 | bytes 4194304 | tf_op jit(solution)/shard_map/pack/pallas_call | solution.py:286
  3.7 0.0 copy-start.1
  3.7 6.6 %all-to-all-start = ((bf16[16,400,128]{2,1,0:T(8,128)(2,1)}), bf16[16,400,128]{2,1,0:T(8,128)(2,1)}, u32[]{:S(2)}, u32[]{:S(2)}) async-start(bf16[16,400,128]{2,1,0:T(8,128)(2,1)} %pack.1), calls=%async_computation | async-start | bytes 3276800 | tf_op jit(solution)/shard_map/all_to_all | solution.py:447
  10.4 0.0 copy-done.1
  10.4 0.0 copy-start.8
  10.4 1.5 %collective-permute-start = (bf16[2048,256]{1,0:T(8,128)(2,1)S(1)}, bf16[2048,256]{1,0:T(8,128)(2,1)S(1)}, u32[]{:S(2)}, u32[]{:S(2)}) collective-permute-start(bf16[2048,256]{1,0:T(8,128)(2,1)S(1)} %copy-done.1), channel_id=1, source_target_pairs={{0,4},{2,6},{4,0},{6,2},{8,12},{10,14},{12,8},{14,10},{16,20},{18,... | collective-permute-start | bytes 3145736 | tf_op jit(solution)/shard_map/ppermute | solution.py:379
  11.8 0.9 fusion
  12.7 1.2 collective-permute-start.1
  13.9 36.4 %collective-permute-done.1.refs_0_ = bf16[1024,256]{1,0:T(8,128)(2,1)S(1)} collective-permute-done((bf16[1024,256]{1,0:T(8,128)(2,1)S(1)}, bf16[1024,256]{1,0:T(8,128)(2,1)S(1)}, u32[]{:S(2)}, u32[]{:S(2)}) %collective-permute-start.1) | collective-permute-done | bytes 524320 | tf_op jit(solution)/shard_map/ppermute | solution.py:379
  50.3 0.0 copy-start.2
  50.3 2.4 %collective-permute-done.refs_2_ = bf16[2048,256]{1,0:T(8,128)(2,1)S(1)} collective-permute-done((bf16[2048,256]{1,0:T(8,128)(2,1)S(1)}, bf16[2048,256]{1,0:T(8,128)(2,1)S(1)}, u32[]{:S(2)}, u32[]{:S(2)}) %collective-permute-start) | collective-permute-done | bytes 1048608 | tf_op jit(solution)/shard_map/ppermute | solution.py:379
  52.7 0.0 all-to-all-done.arrived_ref
  52.7 1.2 collective-permute-start.2
  53.9 0.3 collective-permute-start.3
  54.2 0.0 copy-done.8
  54.3 0.0 copy-done
  54.3 0.1 dynamic-slice_bitcast_fusion.skip_ref
  54.4 0.0 copy-start.6
  54.4 1.1 copy-done.6
  55.5 0.0 copy-start.7
  55.5 1.0 copy-done.7
  56.5 6.4 %gated_conv.1 = bf16[2,8,2,128,128]{4,3,2,1,0:T(8,128)(2,1)} custom-call(bf16[512,512]{1,0:T(8,128)(2,1)S(1)} %copy-done.7, bf16[256,1536]{1,0:T(8,128)(2,1)S(1)} %copy-done.6, bf16[16,400,128]{2,1,0:T(8,128)(2,1)} %all-to-all-done.arrived_ref, f32[9,128]{1,0:T(8,128)S(1)} %constant_dynamic-slice_fusion.taps_ref, f32[1,128]{1,0:T(1,128)S(1)} %dynamic-slice_bitcast_fusion.skip_ref), custom_call_target="tpu_custom_call" | custom-call | flops 1879048192 | bytes 5242880 | tf_op jit(solution)/shard_map/gated_conv/pallas_call | solution.py:313
  63.0 0.0 copy-done.2
  63.0 2.7 %collective-permute-done.2.refs_1_ = bf16[1024,256]{1,0:T(8,128)(2,1)S(1)} collective-permute-done((bf16[1024,256]{1,0:T(8,128)(2,1)}, bf16[1024,256]{1,0:T(8,128)(2,1)S(1)}, u32[]{:S(2)}, u32[]{:S(2)}) %collective-permute-start.2) | collective-permute-done | bytes 524320 | tf_op jit(solution)/shard_map/ppermute | solution.py:379
  65.6 0.0 copy-start.4
  65.6 0.7 collective-permute-done.3.refs_4_
  66.3 0.1 copy-done.4
  66.4 6.2 %all-to-all-start.1 = ((bf16[16,2,128,128]{3,2,1,0:T(8,128)(2,1)}), bf16[16,2,128,128]{3,2,1,0:T(8,128)(2,1)S(1)}, u32[]{:S(2)}, u32[]{:S(2)}) async-start(bf16[16,2,128,128]{3,2,1,0:T(8,128)(2,1)} %bitcast.4), calls=%async_computation.1 | async-start | bytes 2097152 | tf_op jit(solution)/shard_map/all_to_all | solution.py:462
  72.6 0.2 collective-permute-start.4
  72.8 0.3 collective-permute-start.5
  73.2 1.4 %collective-permute-start.10 = (bf16[1024,256]{1,0:T(8,128)(2,1)}, bf16[1024,256]{1,0:T(8,128)(2,1)}, u32[]{:S(2)}, u32[]{:S(2)}) collective-permute-start(bf16[1024,256]{1,0:T(8,128)(2,1)} %copy-done.4), channel_id=1, source_target_pairs={{0,4},{2,6},{4,0},{6,2},{8,12},{10,14},{12,8},{14,10},{16,20},{18,... | collective-permute-start | bytes 1572872 | tf_op jit(solution)/shard_map/ppermute | solution.py:379
  74.5 0.6 collective-permute-start.9
  75.2 0.0 collective-permute-start.8
  75.2 0.3 collective-permute-done.4.refs_1_
  75.4 0.3 collective-permute-start.11
  75.7 1.2 collective-permute-done.5.refs_3_
  76.9 18.9 %all-to-all-done.1 = bf16[16,2,128,128]{3,2,1,0:T(8,128)(2,1)S(1)} async-done(((bf16[16,2,128,128]{3,2,1,0:T(8,128)(2,1)}), bf16[16,2,128,128]{3,2,1,0:T(8,128)(2,1)S(1)}, u32[]{:S(2)}, u32[]{:S(2)}) %all-to-all-start.1) | async-done | bytes 1048608 | tf_op jit(solution)/shard_map/all_to_all | solution.py:462
  95.8 0.0 copy-start.3
  95.8 0.0 copy-start.5
  95.8 3.7 %project.2 = (bf16[128,1024]{1,0:T(8,128)(2,1)}, bf16[128,1024]{1,0:T(8,128)(2,1)S(1)}) custom-call(s32[1]{0:T(128)} %bitcast.1.own_ref, bf16[16,256,128]{2,1,0:T(8,128)(2,1)S(1)} %bitcast.7, bf16[2048,256]{1,0:T(8,128)(2,1)S(1)} %copy-done.1, bf16[2048,256]{1,0:T(8,128)(2,1)} %collective-permute-done.4.refs_1_, ...), custom_call_target="tpu_custom_call" | custom-call | flops 1073741824 | bytes 6291456 | tf_op jit(solution)/shard_map/project/pallas_call | solution.py:340
  99.5 0.0 collective-permute-done.10.refs_5_
  99.5 0.0 collective-permute-start.12
  99.5 6.5 %collective-permute-start.6 = (bf16[128,1024]{1,0:T(8,128)(2,1)}, bf16[128,1024]{1,0:T(8,128)(2,1)S(1)}, u32[]{:S(2)}, u32[]{:S(2)}) collective-permute-start(bf16[128,1024]{1,0:T(8,128)(2,1)} %get-tuple-element.29), channel_id=1, source_target_pairs={{0,0},{1,16},{2,2},{3,18},{4,4},{5,20},{6,6},{7,22},{8,8},{9,24},{... | collective-permute-start | bytes 786440 | tf_op jit(solution)/shard_map/ppermute | solution.py:426
  106.0 0.0 collective-permute-done.8.refs_2_
  106.1 0.1 collective-permute-start.7
  106.1 0.0 collective-permute-done.9.refs_3_
  106.1 0.0 collective-permute-done.11.refs_6_
  106.1 0.0 collective-permute-done.12.refs_7_
  106.1 0.0 copy-done.3
  106.2 0.0 copy-done.5
  106.2 3.0 %project.3 = (bf16[128,1024]{1,0:T(8,128)(2,1)S(1)}, bf16[128,1024]{1,0:T(8,128)(2,1)S(1)}) custom-call(s32[1]{0:T(128)} %bitcast.1.own_ref, bf16[16,256,128]{2,1,0:T(8,128)(2,1)S(1)} %bitcast.8, bf16[1024,256]{1,0:T(8,128)(2,1)S(1)} %copy-done.3, bf16[1024,256]{1,0:T(8,128)(2,1)S(1)} %copy-done.5, bf16[1024,256]{1,0:T(8,128)(2,1)} %collective-permute-done.8.refs_2_, ...), custom_call_target="tpu_custom_call" | custom-call | flops 1073741824 | bytes 6291456 | tf_op jit(solution)/shard_map/project/pallas_call | solution.py:340
  109.2 2.7 %collective-permute-start.13 = (bf16[128,1024]{1,0:T(8,128)(2,1)S(1)}, bf16[128,1024]{1,0:T(8,128)(2,1)S(1)}, u32[]{:S(2)}, u32[]{:S(2)}) collective-permute-start(bf16[128,1024]{1,0:T(8,128)(2,1)S(1)} %get-tuple-element.35), channel_id=1, source_target_pairs={{0,0},{1,16},{2,2},{3,18},{4,4},{5,20},{6,6},{7,22},{8,8},{9,24},{... | collective-permute-start | bytes 786440 | tf_op jit(solution)/shard_map/ppermute | solution.py:426
  112.0 0.1 collective-permute-start.14
  112.0 12.1 %collective-permute-done.6.refs_0_ = bf16[128,1024]{1,0:T(8,128)(2,1)S(1)} collective-permute-done((bf16[128,1024]{1,0:T(8,128)(2,1)}, bf16[128,1024]{1,0:T(8,128)(2,1)S(1)}, u32[]{:S(2)}, u32[]{:S(2)}) %collective-permute-start.6) | collective-permute-done | bytes 262176 | tf_op jit(solution)/shard_map/ppermute | solution.py:426
  124.2 0.8 collective-permute-done.7.refs_1_
  124.9 4.9 %collective-permute-done.13.refs_2_ = bf16[128,1024]{1,0:T(8,128)(2,1)S(1)} collective-permute-done((bf16[128,1024]{1,0:T(8,128)(2,1)S(1)}, bf16[128,1024]{1,0:T(8,128)(2,1)S(1)}, u32[]{:S(2)}, u32[]{:S(2)}) %collective-permute-start.13) | collective-permute-done | bytes 262176 | tf_op jit(solution)/shard_map/ppermute | solution.py:426
  129.8 0.8 collective-permute-done.14.refs_3_
  130.5 0.9 finish.1
  (2 shorter events, 0.0 us)
Async XLA Ops:
  0.0 54.3 %copy-start = (f32[2048]{0:T(1024)S(1)}, f32[2048]{0:T(1024)}, u32[]{:S(2)}) copy-start(f32[2048]{0:T(1024)} %param.10) | copy-start | bytes 24580
  3.7 6.6 %copy-start.1 = (bf16[2048,256]{1,0:T(8,128)(2,1)S(1)}, bf16[2048,256]{1,0:T(8,128)(2,1)}, u32[]{:S(2)}) copy-start(bf16[2048,256]{1,0:T(8,128)(2,1)} %refs_0_) | copy-start | bytes 3145732
  3.7 49.0 %all-to-all-start = ((bf16[16,400,128]{2,1,0:T(8,128)(2,1)}), bf16[16,400,128]{2,1,0:T(8,128)(2,1)}, u32[]{:S(2)}, u32[]{:S(2)}) async-start(bf16[16,400,128]{2,1,0:T(8,128)(2,1)} %pack.1), calls=%async_computation | async-start | bytes 3276800 | tf_op jit(solution)/shard_map/all_to_all | solution.py:447
  10.4 43.9 %copy-start.8 = (f32[3,3,2048]{2,1,0:T(4,128)S(1)}, f32[3,3,2048]{2,1,0:T(4,128)}, u32[]{:S(2)}) copy-start(f32[3,3,2048]{2,1,0:T(4,128)} %taps_ref.1) | copy-start | bytes 221188
  10.4 42.4 %collective-permute-start = (bf16[2048,256]{1,0:T(8,128)(2,1)S(1)}, bf16[2048,256]{1,0:T(8,128)(2,1)S(1)}, u32[]{:S(2)}, u32[]{:S(2)}) collective-permute-start(bf16[2048,256]{1,0:T(8,128)(2,1)S(1)} %copy-done.1), channel_id=1, source_target_pairs={{0,4},{2,6},{4,0},{6,2},{8,12},{10,14},{12,8},{14,10},{16,20},{18,... | collective-permute-start | bytes 3145736 | tf_op jit(solution)/shard_map/ppermute | solution.py:379
  12.7 37.6 %collective-permute-start.1 = (bf16[1024,256]{1,0:T(8,128)(2,1)S(1)}, bf16[1024,256]{1,0:T(8,128)(2,1)S(1)}, u32[]{:S(2)}, u32[]{:S(2)}) collective-permute-start(bf16[1024,256]{1,0:T(8,128)(2,1)S(1)} %get-tuple-element.38), channel_id=1, source_target_pairs={{0,8},{2,10},{4,12},{6,14},{8,0},{10,2},{12,4},{14,6},{16,24},{18,... | collective-permute-start | bytes 1572872 | tf_op jit(solution)/shard_map/ppermute | solution.py:379
  50.3 12.6 %copy-start.2 = (bf16[1024,256]{1,0:T(8,128)(2,1)}, bf16[1024,256]{1,0:T(8,128)(2,1)S(1)}, u32[]{:S(2)}) copy-start(bf16[1024,256]{1,0:T(8,128)(2,1)S(1)} %collective-permute-done.1.refs_0_) | copy-start | bytes 1572868
  52.7 12.9 %collective-permute-start.2 = (bf16[1024,256]{1,0:T(8,128)(2,1)}, bf16[1024,256]{1,0:T(8,128)(2,1)S(1)}, u32[]{:S(2)}, u32[]{:S(2)}) collective-permute-start(bf16[1024,256]{1,0:T(8,128)(2,1)} %get-tuple-element.25), channel_id=1, source_target_pairs={{0,8},{2,10},{4,12},{6,14},{8,0},{10,2},{12,4},{14,6},{16,24},{18,... | collective-permute-start | bytes 1572872 | tf_op jit(solution)/shard_map/ppermute | solution.py:379
  53.9 12.4 %collective-permute-start.3 = (bf16[1024,256]{1,0:T(8,128)(2,1)S(1)}, bf16[1024,256]{1,0:T(8,128)(2,1)}, u32[]{:S(2)}, u32[]{:S(2)}) collective-permute-start(bf16[1024,256]{1,0:T(8,128)(2,1)S(1)} %collective-permute-done.1.refs_0_), channel_id=1, source_target_pairs={{0,4},{2,6},{4,0},{6,2},{8,12},{10,14},{12,8},{14,10},{16,20},{18,... | collective-permute-start | bytes 1572872 | tf_op jit(solution)/shard_map/ppermute | solution.py:379
  54.4 1.1 copy-start.6
  55.5 1.0 copy-start.7
  65.6 0.8 copy-start.4
  66.4 29.4 %all-to-all-start.1 = ((bf16[16,2,128,128]{3,2,1,0:T(8,128)(2,1)}), bf16[16,2,128,128]{3,2,1,0:T(8,128)(2,1)S(1)}, u32[]{:S(2)}, u32[]{:S(2)}) async-start(bf16[16,2,128,128]{3,2,1,0:T(8,128)(2,1)} %bitcast.4), calls=%async_computation.1 | async-start | bytes 2097152 | tf_op jit(solution)/shard_map/all_to_all | solution.py:462
  72.6 2.8 %collective-permute-start.4 = (bf16[2048,256]{1,0:T(8,128)(2,1)S(1)}, bf16[2048,256]{1,0:T(8,128)(2,1)}, u32[]{:S(2)}, u32[]{:S(2)}) collective-permute-start(bf16[2048,256]{1,0:T(8,128)(2,1)S(1)} %copy-done.1), channel_id=1, source_target_pairs={{0,2},{2,0},{4,6},{6,4},{8,10},{10,8},{12,14},{14,12},{16,18},{18,... | collective-permute-start | bytes 3145736 | tf_op jit(solution)/shard_map/ppermute | solution.py:379
  72.8 4.1 %collective-permute-start.5 = (bf16[2048,256]{1,0:T(8,128)(2,1)S(1)}, bf16[2048,256]{1,0:T(8,128)(2,1)}, u32[]{:S(2)}, u32[]{:S(2)}) collective-permute-start(bf16[2048,256]{1,0:T(8,128)(2,1)S(1)} %collective-permute-done.refs_2_), channel_id=1, source_target_pairs={{0,2},{2,0},{4,6},{6,4},{8,10},{10,8},{12,14},{14,12},{16,18},{18,... | collective-permute-start | bytes 3145736 | tf_op jit(solution)/shard_map/ppermute | solution.py:379
  73.2 26.4 %collective-permute-start.10 = (bf16[1024,256]{1,0:T(8,128)(2,1)}, bf16[1024,256]{1,0:T(8,128)(2,1)}, u32[]{:S(2)}, u32[]{:S(2)}) collective-permute-start(bf16[1024,256]{1,0:T(8,128)(2,1)} %copy-done.4), channel_id=1, source_target_pairs={{0,4},{2,6},{4,0},{6,2},{8,12},{10,14},{12,8},{14,10},{16,20},{18,... | collective-permute-start | bytes 1572872 | tf_op jit(solution)/shard_map/ppermute | solution.py:379
  74.5 31.6 %collective-permute-start.9 = (bf16[1024,256]{1,0:T(8,128)(2,1)}, bf16[1024,256]{1,0:T(8,128)(2,1)}, u32[]{:S(2)}, u32[]{:S(2)}) collective-permute-start(bf16[1024,256]{1,0:T(8,128)(2,1)} %copy-done.4), channel_id=1, source_target_pairs={{0,2},{2,0},{4,6},{6,4},{8,10},{10,8},{12,14},{14,12},{16,18},{18,... | collective-permute-start | bytes 1572872 | tf_op jit(solution)/shard_map/ppermute | solution.py:379
  75.2 30.9 %collective-permute-start.8 = (bf16[1024,256]{1,0:T(8,128)(2,1)}, bf16[1024,256]{1,0:T(8,128)(2,1)}, u32[]{:S(2)}, u32[]{:S(2)}) collective-permute-start(bf16[1024,256]{1,0:T(8,128)(2,1)} %copy-done.2), channel_id=1, source_target_pairs={{0,2},{2,0},{4,6},{6,4},{8,10},{10,8},{12,14},{14,12},{16,18},{18,... | collective-permute-start | bytes 1572872 | tf_op jit(solution)/shard_map/ppermute | solution.py:379
  75.4 30.7 %collective-permute-start.11 = (bf16[1024,256]{1,0:T(8,128)(2,1)}, bf16[1024,256]{1,0:T(8,128)(2,1)}, u32[]{:S(2)}, u32[]{:S(2)}) collective-permute-start(bf16[1024,256]{1,0:T(8,128)(2,1)} %collective-permute-done.3.refs_4_), channel_id=1, source_target_pairs={{0,2},{2,0},{4,6},{6,4},{8,10},{10,8},{12,14},{14,12},{16,18},{18,... | collective-permute-start | bytes 1572872 | tf_op jit(solution)/shard_map/ppermute | solution.py:379
  95.8 10.4 %copy-start.3 = (bf16[1024,256]{1,0:T(8,128)(2,1)S(1)}, bf16[1024,256]{1,0:T(8,128)(2,1)}, u32[]{:S(2)}) copy-start(bf16[1024,256]{1,0:T(8,128)(2,1)} %copy-done.2) | copy-start | bytes 1572868
  95.8 10.4 %copy-start.5 = (bf16[1024,256]{1,0:T(8,128)(2,1)S(1)}, bf16[1024,256]{1,0:T(8,128)(2,1)}, u32[]{:S(2)}) copy-start(bf16[1024,256]{1,0:T(8,128)(2,1)} %copy-done.4) | copy-start | bytes 1572868
  99.5 6.6 %collective-permute-start.12 = (bf16[1024,256]{1,0:T(8,128)(2,1)}, bf16[1024,256]{1,0:T(8,128)(2,1)S(1)}, u32[]{:S(2)}, u32[]{:S(2)}) collective-permute-start(bf16[1024,256]{1,0:T(8,128)(2,1)} %collective-permute-done.10.refs_5_), channel_id=1, source_target_pairs={{0,2},{2,0},{4,6},{6,4},{8,10},{10,8},{12,14},{14,12},{16,18},{18,... | collective-permute-start | bytes 1572872 | tf_op jit(solution)/shard_map/ppermute | solution.py:379
  99.5 24.6 %collective-permute-start.6 = (bf16[128,1024]{1,0:T(8,128)(2,1)}, bf16[128,1024]{1,0:T(8,128)(2,1)S(1)}, u32[]{:S(2)}, u32[]{:S(2)}) collective-permute-start(bf16[128,1024]{1,0:T(8,128)(2,1)} %get-tuple-element.29), channel_id=1, source_target_pairs={{0,0},{1,16},{2,2},{3,18},{4,4},{5,20},{6,6},{7,22},{8,8},{9,24},{... | collective-permute-start | bytes 786440 | tf_op jit(solution)/shard_map/ppermute | solution.py:426
  106.1 18.9 %collective-permute-start.7 = (bf16[128,1024]{1,0:T(8,128)(2,1)S(1)}, bf16[128,1024]{1,0:T(8,128)(2,1)S(1)}, u32[]{:S(2)}, u32[]{:S(2)}) collective-permute-start(bf16[128,1024]{1,0:T(8,128)(2,1)S(1)} %get-tuple-element.30), channel_id=1, source_target_pairs={{0,16},{1,0},{2,18},{3,2},{4,20},{5,4},{6,22},{7,6},{8,24},{9,8},{... | collective-permute-start | bytes 786440 | tf_op jit(solution)/shard_map/ppermute | solution.py:426
  109.2 20.6 %collective-permute-start.13 = (bf16[128,1024]{1,0:T(8,128)(2,1)S(1)}, bf16[128,1024]{1,0:T(8,128)(2,1)S(1)}, u32[]{:S(2)}, u32[]{:S(2)}) collective-permute-start(bf16[128,1024]{1,0:T(8,128)(2,1)S(1)} %get-tuple-element.35), channel_id=1, source_target_pairs={{0,0},{1,16},{2,2},{3,18},{4,4},{5,20},{6,6},{7,22},{8,8},{9,24},{... | collective-permute-start | bytes 786440 | tf_op jit(solution)/shard_map/ppermute | solution.py:426
  112.0 18.6 %collective-permute-start.14 = (bf16[128,1024]{1,0:T(8,128)(2,1)S(1)}, bf16[128,1024]{1,0:T(8,128)(2,1)S(1)}, u32[]{:S(2)}, u32[]{:S(2)}) collective-permute-start(bf16[128,1024]{1,0:T(8,128)(2,1)S(1)} %get-tuple-element.36), channel_id=1, source_target_pairs={{0,16},{1,0},{2,18},{3,2},{4,20},{5,4},{6,22},{7,6},{8,24},{9,8},{... | collective-permute-start | bytes 786440 | tf_op jit(solution)/shard_map/ppermute | solution.py:426

commit v3 on v2

--- a/solution.py
+++ b/solution.py
@@ -379,13 +379,21 @@
     return lax.ppermute(value, "ctx", pairs)
 
 
-def weights_on_the_way(out_weight):
-    upper = out_weight[: out_weight.shape[0] // 2]
-    return {0: [out_weight], 2: [from_partner(out_weight, 2)], 4: [from_partner(upper, 4)]}
-
-
-def weights_passed_on(pieces, lower):
-    return {**pieces, 4: pieces[4] + [from_partner(lower, 4)], 6: [from_partner(pieces[4][0], 2)]}
+def after(values, *others):
+    return lax.optimization_barrier((values, others))[0]
+
+
+def weights_from_chips(out_weight, packed, arrived):
+    cut = out_weight.shape[0] // 16 * 7
+    own = after(out_weight, packed)
+    x_piece = from_partner(own, 2)
+    z_first, rest = after((from_partner(own[:cut], 4), own[cut:]), arrived)
+    return {
+        0: [out_weight],
+        2: [x_piece],
+        4: [z_first, from_partner(rest, 4)],
+        6: [from_partner(z_first, 2)],
+    }
 
 
 def weights_between_cores(pieces):
@@ -446,11 +454,7 @@
     packed = pack(qkv_in.transpose(1, 0, 2), short_taps, long_filter, peers)
     arrived = lax.all_to_all(packed, "ctx", split_axis=0, concat_axis=0, tiled=True)
     if copies == 2:
-        own_weight, _ = lax.optimization_barrier((out_weight, packed))
-        pieces = weights_on_the_way(own_weight)
-        lower = own_weight[own_weight.shape[0] // 2 :]
-        (pieces, lower), _ = lax.optimization_barrier(((pieces, lower), arrived))
-        pieces = weights_passed_on(pieces, lower)
+        pieces = weights_from_chips(out_weight, packed, arrived)
 
     taps = own_columns(short_taps.reshape(-1, channel_count), lanes)
     skip = own_columns(skip_gain[None, :], lanes)

time: 132 us -> 131 us (level)
  waiting for transfers between devices: 81.1 us -> 77.4 us
  starting transfers between devices: 29.1 us -> 31.2 us
    ppermute x11, waiting for transfers between devices: 43.7 us -> 40.2 us  [from_partner(): return lax.ppermute(value, 'ctx', pairs)]
  transfers between devices with their start and end apart: 17 -> 17, of which waited for: 11 -> 10; matrix products, arithmetic and copies ran while one was open for 1% -> 1% of each run, Pallas kernels for 10% -> 10%
where the time goes in v3:
time: 131 us; the launch traced here: 130 us
  waiting for transfers between devices  77.4 us (59%)
  starting transfers between devices  31.2 us (24%)
  Pallas kernels  17.6 us (13%)
  local copies, waits for them, and re-layouts  4.02 us (3%)
    ppermute x11, waiting for transfers between devices, from_partner(): return lax.ppermute(value, 'ctx', pairs)  40.2 us
    all_to_all x1, waiting for transfers between devices, body(): lax.all_to_all(by_target, 'ctx', split_axis=0, concat_axis=0, tiled=True)  18.9 us
    ppermute x4, waiting for transfers between devices, to_their_place(): return lax.ppermute(partial, ('ctx', 'tp'), pairs)  18.3 us
    ppermute x4, starting transfers between devices, to_their_place(): return lax.ppermute(partial, ('ctx', 'tp'), pairs)  9.88 us
    ppermute x11, starting transfers between devices, from_partner(): return lax.ppermute(value, 'ctx', pairs)  8.07 us
    all_to_all x1, starting transfers between devices, body(): lax.all_to_all(by_target, 'ctx', split_axis=0, concat_axis=0, tiled=True)  6.67 us
    all_to_all x1, starting transfers between devices, body(): lax.all_to_all(packed, 'ctx', split_axis=0, concat_axis=0, tiled=True)  6.62 us
    pallas_call x2, Pallas kernels, project(): pl.pallas_call(functools.partial(project_kernel, [len(parts) for parts in...  6.61 us
  transfers between devices with their start and end apart: 17, of which 10 were waited for; matrix products, arithmetic and copies ran while one was open for 1% of the time, Pallas kernels for 10%

profile of v3, /device:TPU:5, one launch (start us, length us, event | category | flops | bytes accessed | tf_op | source)
XLA Modules:
  0.0 130.4 jit_solution(919019685068753923)
XLA Ops:
  0.0 0.0 copy-start
  0.0 3.7 %pack.1 = bf16[16,400,128]{2,1,0:T(8,128)(2,1)} custom-call(bf16[3,128,2048]{2,1,0:T(8,128)(2,1)} %bitcast.9, f32[3,3,2048]{2,1,0:T(4,128)} %taps_ref.1, f32[128,2048]{1,0:T(8,128)} %filter_ref.1), custom_call_target="tpu_custom_call" | custom-call | flops 4194304 | bytes 4194304 | tf_op jit(solution)/shard_map/pack/pallas_call | solution.py:286
  3.7 0.0 copy-start.1
  3.7 6.6 %all-to-all-start = ((bf16[16,400,128]{2,1,0:T(8,128)(2,1)}), bf16[16,400,128]{2,1,0:T(8,128)(2,1)}, u32[]{:S(2)}, u32[]{:S(2)}) async-start(bf16[16,400,128]{2,1,0:T(8,128)(2,1)} %pack.1), calls=%async_computation | async-start | bytes 3276800 | tf_op jit(solution)/shard_map/all_to_all | solution.py:455
  10.3 0.0 copy-done.1
  10.4 0.0 copy-start.8
  10.4 1.5 %collective-permute-start.1 = (bf16[896,256]{1,0:T(8,128)(2,1)S(1)}, bf16[896,256]{1,0:T(8,128)(2,1)S(1)}, u32[]{:S(2)}, u32[]{:S(2)}) collective-permute-start(bf16[896,256]{1,0:T(8,128)(2,1)S(1)} %slice.6), channel_id=1, source_target_pairs={{0,8},{2,10},{4,12},{6,14},{8,0},{10,2},{12,4},{14,6},{16,24},{18,... | collective-permute-start | bytes 1376264 | tf_op jit(solution)/shard_map/ppermute | solution.py:379
  11.9 1.2 collective-permute-start
  13.0 0.9 slice.7
  13.9 35.0 %collective-permute-done.1.refs_0_ = bf16[896,256]{1,0:T(8,128)(2,1)S(1)} collective-permute-done((bf16[896,256]{1,0:T(8,128)(2,1)S(1)}, bf16[896,256]{1,0:T(8,128)(2,1)S(1)}, u32[]{:S(2)}, u32[]{:S(2)}) %collective-permute-start.1) | collective-permute-done | bytes 458784 | tf_op jit(solution)/shard_map/ppermute | solution.py:379
  48.9 0.0 copy-start.4
  48.9 0.0 all-to-all-done.arrived_ref
  48.9 0.7 collective-permute-start.2
  49.6 1.4 %collective-permute-start.3 = (bf16[896,256]{1,0:T(8,128)(2,1)S(1)}, bf16[896,256]{1,0:T(8,128)(2,1)}, u32[]{:S(2)}, u32[]{:S(2)}) collective-permute-start(bf16[896,256]{1,0:T(8,128)(2,1)S(1)} %collective-permute-done.1.refs_0_), channel_id=1, source_target_pairs={{0,4},{2,6},{4,0},{6,2},{8,12},{10,14},{12,8},{14,10},{16,20},{18,... | collective-permute-start | bytes 1376264 | tf_op jit(solution)/shard_map/ppermute | solution.py:379
  51.0 0.0 copy-done.8
  51.0 0.0 copy-done
  51.0 0.1 dynamic-slice_bitcast_fusion.skip_ref
  51.1 0.0 copy-start.6
  51.1 1.1 copy-done.6
  52.3 0.0 copy-start.7
  52.3 1.0 copy-done.7
  53.3 6.4 %gated_conv.1 = bf16[2,8,2,128,128]{4,3,2,1,0:T(8,128)(2,1)} custom-call(bf16[512,512]{1,0:T(8,128)(2,1)S(1)} %copy-done.7, bf16[256,1536]{1,0:T(8,128)(2,1)S(1)} %copy-done.6, bf16[16,400,128]{2,1,0:T(8,128)(2,1)} %all-to-all-done.arrived_ref, f32[9,128]{1,0:T(8,128)S(1)} %constant_dynamic-slice_fusion.taps_ref, f32[1,128]{1,0:T(1,128)S(1)} %dynamic-slice_bitcast_fusion.skip_ref), custom_call_target="tpu_custom_call" | custom-call | flops 1879048192 | bytes 5242880 | tf_op jit(solution)/shard_map/gated_conv/pallas_call | solution.py:313
  59.7 0.0 copy-done.4
  59.7 0.0 collective-permute-done.refs_2_
  59.7 3.0 %collective-permute-done.3.refs_4_ = bf16[896,256]{1,0:T(8,128)(2,1)} collective-permute-done((bf16[896,256]{1,0:T(8,128)(2,1)S(1)}, bf16[896,256]{1,0:T(8,128)(2,1)}, u32[]{:S(2)}, u32[]{:S(2)}) %collective-permute-start.3) | collective-permute-done | bytes 458784 | tf_op jit(solution)/shard_map/ppermute | solution.py:379
  62.7 0.5 collective-permute-done.2.refs_1_
  63.1 0.0 copy-start.2
  63.1 0.8 copy-done.2
  64.0 6.7 %all-to-all-start.1 = ((bf16[16,2,128,128]{3,2,1,0:T(8,128)(2,1)}), bf16[16,2,128,128]{3,2,1,0:T(8,128)(2,1)S(1)}, u32[]{:S(2)}, u32[]{:S(2)}) async-start(bf16[16,2,128,128]{3,2,1,0:T(8,128)(2,1)} %bitcast.4), calls=%async_computation.1 | async-start | bytes 2097152 | tf_op jit(solution)/shard_map/all_to_all | solution.py:466
  70.6 0.2 collective-permute-start.4
  70.8 0.3 collective-permute-start.5
  71.1 1.4 %collective-permute-start.10 = (bf16[1152,256]{1,0:T(8,128)(2,1)}, bf16[1152,256]{1,0:T(8,128)(2,1)}, u32[]{:S(2)}, u32[]{:S(2)}) collective-permute-start(bf16[1152,256]{1,0:T(8,128)(2,1)} %copy-done.2), channel_id=1, source_target_pairs={{0,4},{2,6},{4,0},{6,2},{8,12},{10,14},{12,8},{14,10},{16,20},{18,... | collective-permute-start | bytes 1769480 | tf_op jit(solution)/shard_map/ppermute | solution.py:379
  72.5 0.6 collective-permute-start.9
  73.2 0.3 collective-permute-done.4.refs_1_
  73.4 1.5 %collective-permute-done.5.refs_3_ = bf16[2048,256]{1,0:T(8,128)(2,1)} collective-permute-done((bf16[2048,256]{1,0:T(8,128)(2,1)S(1)}, bf16[2048,256]{1,0:T(8,128)(2,1)}, u32[]{:S(2)}, u32[]{:S(2)}) %collective-permute-start.5) | collective-permute-done | bytes 1048608 | tf_op jit(solution)/shard_map/ppermute | solution.py:379
  74.9 18.9 %all-to-all-done.1 = bf16[16,2,128,128]{3,2,1,0:T(8,128)(2,1)S(1)} async-done(((bf16[16,2,128,128]{3,2,1,0:T(8,128)(2,1)}), bf16[16,2,128,128]{3,2,1,0:T(8,128)(2,1)S(1)}, u32[]{:S(2)}, u32[]{:S(2)}) %all-to-all-start.1) | async-done | bytes 1048608 | tf_op jit(solution)/shard_map/all_to_all | solution.py:466
  93.8 0.0 copy-start.5
  93.8 0.0 copy-start.3
  93.8 3.7 %project.2 = (bf16[128,1024]{1,0:T(8,128)(2,1)}, bf16[128,1024]{1,0:T(8,128)(2,1)S(1)}) custom-call(s32[1]{0:T(128)} %bitcast.1.own_ref, bf16[16,256,128]{2,1,0:T(8,128)(2,1)S(1)} %bitcast.7, bf16[2048,256]{1,0:T(8,128)(2,1)S(1)} %copy-done.1, bf16[2048,256]{1,0:T(8,128)(2,1)} %collective-permute-done.4.refs_1_, ...), custom_call_target="tpu_custom_call" | custom-call | flops 1073741824 | bytes 6291456 | tf_op jit(solution)/shard_map/project/pallas_call | solution.py:340
  97.5 0.0 collective-permute-done.10.refs_5_
  97.5 0.3 collective-permute-start.12
  97.8 0.0 copy-done.5
  97.8 0.2 collective-permute-start.8
  98.0 0.3 collective-permute-start.11
  98.4 6.3 %collective-permute-start.6 = (bf16[128,1024]{1,0:T(8,128)(2,1)}, bf16[128,1024]{1,0:T(8,128)(2,1)S(1)}, u32[]{:S(2)}, u32[]{:S(2)}) collective-permute-start(bf16[128,1024]{1,0:T(8,128)(2,1)} %get-tuple-element.25), channel_id=1, source_target_pairs={{0,0},{1,16},{2,2},{3,18},{4,4},{5,20},{6,6},{7,22},{8,8},{9,24},{... | collective-permute-start | bytes 786440 | tf_op jit(solution)/shard_map/ppermute | solution.py:434
  104.7 0.0 collective-permute-done.8.refs_2_
  104.7 0.1 collective-permute-start.7
  104.7 0.0 collective-permute-done.11.refs_6_
  104.8 0.0 collective-permute-done.9.refs_3_
  104.8 0.0 collective-permute-done.12.refs_7_
  104.8 0.0 copy-done.3
  104.8 2.9 %project.3 = (bf16[128,1024]{1,0:T(8,128)(2,1)S(1)}, bf16[128,1024]{1,0:T(8,128)(2,1)S(1)}) custom-call(s32[1]{0:T(128)} %bitcast.1.own_ref, bf16[16,256,128]{2,1,0:T(8,128)(2,1)S(1)} %bitcast.8, bf16[896,256]{1,0:T(8,128)(2,1)S(1)} %copy-done.5, bf16[1152,256]{1,0:T(8,128)(2,1)S(1)} %copy-done.3, bf16[896,256]{1,0:T(8,128)(2,1)S(1)} %collective-permute-done.8.refs_2_, ...), custom_call_target="tpu_custom_call" | custom-call | flops 1073741824 | bytes 6291456 | tf_op jit(solution)/shard_map/project/pallas_call | solution.py:340
  107.7 3.5 %collective-permute-start.13 = (bf16[128,1024]{1,0:T(8,128)(2,1)S(1)}, bf16[128,1024]{1,0:T(8,128)(2,1)S(1)}, u32[]{:S(2)}, u32[]{:S(2)}) collective-permute-start(bf16[128,1024]{1,0:T(8,128)(2,1)S(1)} %get-tuple-element.31), channel_id=1, source_target_pairs={{0,0},{1,16},{2,2},{3,18},{4,4},{5,20},{6,6},{7,22},{8,8},{9,24},{... | collective-permute-start | bytes 786440 | tf_op jit(solution)/shard_map/ppermute | solution.py:434
  111.1 0.1 collective-permute-start.14
  111.2 11.5 %collective-permute-done.6.refs_0_ = bf16[128,1024]{1,0:T(8,128)(2,1)S(1)} collective-permute-done((bf16[128,1024]{1,0:T(8,128)(2,1)}, bf16[128,1024]{1,0:T(8,128)(2,1)S(1)}, u32[]{:S(2)}, u32[]{:S(2)}) %collective-permute-start.6) | collective-permute-done | bytes 262176 | tf_op jit(solution)/shard_map/ppermute | solution.py:434
  122.7 1.2 collective-permute-done.7.refs_1_
  123.9 4.4 %collective-permute-done.13.refs_2_ = bf16[128,1024]{1,0:T(8,128)(2,1)S(1)} collective-permute-done((bf16[128,1024]{1,0:T(8,128)(2,1)S(1)}, bf16[128,1024]{1,0:T(8,128)(2,1)S(1)}, u32[]{:S(2)}, u32[]{:S(2)}) %collective-permute-start.13) | collective-permute-done | bytes 262176 | tf_op jit(solution)/shard_map/ppermute | solution.py:434
  128.3 1.2 collective-permute-done.14.refs_3_
  129.5 0.9 finish.1
  (3 shorter events, 0.1 us)
Async XLA Ops:
  0.0 51.0 %copy-start = (f32[2048]{0:T(1024)S(1)}, f32[2048]{0:T(1024)}, u32[]{:S(2)}) copy-start(f32[2048]{0:T(1024)} %param.10) | copy-start | bytes 24580
  3.7 6.6 %copy-start.1 = (bf16[2048,256]{1,0:T(8,128)(2,1)S(1)}, bf16[2048,256]{1,0:T(8,128)(2,1)}, u32[]{:S(2)}) copy-start(bf16[2048,256]{1,0:T(8,128)(2,1)} %refs_0_) | copy-start | bytes 3145732
  3.7 45.2 %all-to-all-start = ((bf16[16,400,128]{2,1,0:T(8,128)(2,1)}), bf16[16,400,128]{2,1,0:T(8,128)(2,1)}, u32[]{:S(2)}, u32[]{:S(2)}) async-start(bf16[16,400,128]{2,1,0:T(8,128)(2,1)} %pack.1), calls=%async_computation | async-start | bytes 3276800 | tf_op jit(solution)/shard_map/all_to_all | solution.py:455
  10.4 40.6 %copy-start.8 = (f32[3,3,2048]{2,1,0:T(4,128)S(1)}, f32[3,3,2048]{2,1,0:T(4,128)}, u32[]{:S(2)}) copy-start(f32[3,3,2048]{2,1,0:T(4,128)} %taps_ref.1) | copy-start | bytes 221188
  10.4 38.5 %collective-permute-start.1 = (bf16[896,256]{1,0:T(8,128)(2,1)S(1)}, bf16[896,256]{1,0:T(8,128)(2,1)S(1)}, u32[]{:S(2)}, u32[]{:S(2)}) collective-permute-start(bf16[896,256]{1,0:T(8,128)(2,1)S(1)} %slice.6), channel_id=1, source_target_pairs={{0,8},{2,10},{4,12},{6,14},{8,0},{10,2},{12,4},{14,6},{16,24},{18,... | collective-permute-start | bytes 1376264 | tf_op jit(solution)/shard_map/ppermute | solution.py:379
  11.9 47.9 %collective-permute-start = (bf16[2048,256]{1,0:T(8,128)(2,1)S(1)}, bf16[2048,256]{1,0:T(8,128)(2,1)S(1)}, u32[]{:S(2)}, u32[]{:S(2)}) collective-permute-start(bf16[2048,256]{1,0:T(8,128)(2,1)S(1)} %copy-done.1), channel_id=1, source_target_pairs={{0,4},{2,6},{4,0},{6,2},{8,12},{10,14},{12,8},{14,10},{16,20},{18,... | collective-permute-start | bytes 3145736 | tf_op jit(solution)/shard_map/ppermute | solution.py:379
  48.9 10.8 %copy-start.4 = (bf16[896,256]{1,0:T(8,128)(2,1)}, bf16[896,256]{1,0:T(8,128)(2,1)S(1)}, u32[]{:S(2)}) copy-start(bf16[896,256]{1,0:T(8,128)(2,1)S(1)} %collective-permute-done.1.refs_0_) | copy-start | bytes 1376260
  48.9 14.2 %collective-permute-start.2 = (bf16[1152,256]{1,0:T(8,128)(2,1)}, bf16[1152,256]{1,0:T(8,128)(2,1)S(1)}, u32[]{:S(2)}, u32[]{:S(2)}) collective-permute-start(bf16[1152,256]{1,0:T(8,128)(2,1)} %slice.7), channel_id=1, source_target_pairs={{0,8},{2,10},{4,12},{6,14},{8,0},{10,2},{12,4},{14,6},{16,24},{18,... | collective-permute-start | bytes 1769480 | tf_op jit(solution)/shard_map/ppermute | solution.py:379
  49.6 13.1 %collective-permute-start.3 = (bf16[896,256]{1,0:T(8,128)(2,1)S(1)}, bf16[896,256]{1,0:T(8,128)(2,1)}, u32[]{:S(2)}, u32[]{:S(2)}) collective-permute-start(bf16[896,256]{1,0:T(8,128)(2,1)S(1)} %collective-permute-done.1.refs_0_), channel_id=1, source_target_pairs={{0,4},{2,6},{4,0},{6,2},{8,12},{10,14},{12,8},{14,10},{16,20},{18,... | collective-permute-start | bytes 1376264 | tf_op jit(solution)/shard_map/ppermute | solution.py:379
  51.1 1.1 copy-start.6
  52.3 1.0 copy-start.7
  63.1 0.8 copy-start.2
  64.0 29.8 %all-to-all-start.1 = ((bf16[16,2,128,128]{3,2,1,0:T(8,128)(2,1)}), bf16[16,2,128,128]{3,2,1,0:T(8,128)(2,1)S(1)}, u32[]{:S(2)}, u32[]{:S(2)}) async-start(bf16[16,2,128,128]{3,2,1,0:T(8,128)(2,1)} %bitcast.4), calls=%async_computation.1 | async-start | bytes 2097152 | tf_op jit(solution)/shard_map/all_to_all | solution.py:466
  70.6 2.8 %collective-permute-start.4 = (bf16[2048,256]{1,0:T(8,128)(2,1)S(1)}, bf16[2048,256]{1,0:T(8,128)(2,1)}, u32[]{:S(2)}, u32[]{:S(2)}) collective-permute-start(bf16[2048,256]{1,0:T(8,128)(2,1)S(1)} %copy-done.1), channel_id=1, source_target_pairs={{0,2},{2,0},{4,6},{6,4},{8,10},{10,8},{12,14},{14,12},{16,18},{18,... | collective-permute-start | bytes 3145736 | tf_op jit(solution)/shard_map/ppermute | solution.py:379
  70.8 4.1 %collective-permute-start.5 = (bf16[2048,256]{1,0:T(8,128)(2,1)S(1)}, bf16[2048,256]{1,0:T(8,128)(2,1)}, u32[]{:S(2)}, u32[]{:S(2)}) collective-permute-start(bf16[2048,256]{1,0:T(8,128)(2,1)S(1)} %collective-permute-done.refs_2_), channel_id=1, source_target_pairs={{0,2},{2,0},{4,6},{6,4},{8,10},{10,8},{12,14},{14,12},{16,18},{18,... | collective-permute-start | bytes 3145736 | tf_op jit(solution)/shard_map/ppermute | solution.py:379
  71.1 26.4 %collective-permute-start.10 = (bf16[1152,256]{1,0:T(8,128)(2,1)}, bf16[1152,256]{1,0:T(8,128)(2,1)}, u32[]{:S(2)}, u32[]{:S(2)}) collective-permute-start(bf16[1152,256]{1,0:T(8,128)(2,1)} %copy-done.2), channel_id=1, source_target_pairs={{0,4},{2,6},{4,0},{6,2},{8,12},{10,14},{12,8},{14,10},{16,20},{18,... | collective-permute-start | bytes 1769480 | tf_op jit(solution)/shard_map/ppermute | solution.py:379
  72.5 32.2 %collective-permute-start.9 = (bf16[1152,256]{1,0:T(8,128)(2,1)}, bf16[1152,256]{1,0:T(8,128)(2,1)}, u32[]{:S(2)}, u32[]{:S(2)}) collective-permute-start(bf16[1152,256]{1,0:T(8,128)(2,1)} %copy-done.2), channel_id=1, source_target_pairs={{0,2},{2,0},{4,6},{6,4},{8,10},{10,8},{12,14},{14,12},{16,18},{18,... | collective-permute-start | bytes 1769480 | tf_op jit(solution)/shard_map/ppermute | solution.py:379
  93.8 4.1 %copy-start.5 = (bf16[896,256]{1,0:T(8,128)(2,1)S(1)}, bf16[896,256]{1,0:T(8,128)(2,1)}, u32[]{:S(2)}) copy-start(bf16[896,256]{1,0:T(8,128)(2,1)} %copy-done.4) | copy-start | bytes 1376260
  93.8 11.0 %copy-start.3 = (bf16[1152,256]{1,0:T(8,128)(2,1)S(1)}, bf16[1152,256]{1,0:T(8,128)(2,1)}, u32[]{:S(2)}) copy-start(bf16[1152,256]{1,0:T(8,128)(2,1)} %copy-done.2) | copy-start | bytes 1769476
  97.5 7.2 %collective-permute-start.12 = (bf16[1152,256]{1,0:T(8,128)(2,1)}, bf16[1152,256]{1,0:T(8,128)(2,1)S(1)}, u32[]{:S(2)}, u32[]{:S(2)}) collective-permute-start(bf16[1152,256]{1,0:T(8,128)(2,1)} %collective-permute-done.10.refs_5_), channel_id=1, source_target_pairs={{0,2},{2,0},{4,6},{6,4},{8,10},{10,8},{12,14},{14,12},{16,18},{18,... | collective-permute-start | bytes 1769480 | tf_op jit(solution)/shard_map/ppermute | solution.py:379
  97.8 6.8 %collective-permute-start.8 = (bf16[896,256]{1,0:T(8,128)(2,1)S(1)}, bf16[896,256]{1,0:T(8,128)(2,1)S(1)}, u32[]{:S(2)}, u32[]{:S(2)}) collective-permute-start(bf16[896,256]{1,0:T(8,128)(2,1)S(1)} %copy-done.5), channel_id=1, source_target_pairs={{0,2},{2,0},{4,6},{6,4},{8,10},{10,8},{12,14},{14,12},{16,18},{18,... | collective-permute-start | bytes 1376264 | tf_op jit(solution)/shard_map/ppermute | solution.py:379
  98.0 6.7 %collective-permute-start.11 = (bf16[896,256]{1,0:T(8,128)(2,1)}, bf16[896,256]{1,0:T(8,128)(2,1)S(1)}, u32[]{:S(2)}, u32[]{:S(2)}) collective-permute-start(bf16[896,256]{1,0:T(8,128)(2,1)} %collective-permute-done.3.refs_4_), channel_id=1, source_target_pairs={{0,2},{2,0},{4,6},{6,4},{8,10},{10,8},{12,14},{14,12},{16,18},{18,... | collective-permute-start | bytes 1376264 | tf_op jit(solution)/shard_map/ppermute | solution.py:379
  98.4 24.4 %collective-permute-start.6 = (bf16[128,1024]{1,0:T(8,128)(2,1)}, bf16[128,1024]{1,0:T(8,128)(2,1)S(1)}, u32[]{:S(2)}, u32[]{:S(2)}) collective-permute-start(bf16[128,1024]{1,0:T(8,128)(2,1)} %get-tuple-element.25), channel_id=1, source_target_pairs={{0,0},{1,16},{2,2},{3,18},{4,4},{5,20},{6,6},{7,22},{8,8},{9,24},{... | collective-permute-start | bytes 786440 | tf_op jit(solution)/shard_map/ppermute | solution.py:434
  104.7 19.2 %collective-permute-start.7 = (bf16[128,1024]{1,0:T(8,128)(2,1)S(1)}, bf16[128,1024]{1,0:T(8,128)(2,1)S(1)}, u32[]{:S(2)}, u32[]{:S(2)}) collective-permute-start(bf16[128,1024]{1,0:T(8,128)(2,1)S(1)} %get-tuple-element.26), channel_id=1, source_target_pairs={{0,16},{1,0},{2,18},{3,2},{4,20},{5,4},{6,22},{7,6},{8,24},{9,8},{... | collective-permute-start | bytes 786440 | tf_op jit(solution)/shard_map/ppermute | solution.py:434
  107.7 20.7 %collective-permute-start.13 = (bf16[128,1024]{1,0:T(8,128)(2,1)S(1)}, bf16[128,1024]{1,0:T(8,128)(2,1)S(1)}, u32[]{:S(2)}, u32[]{:S(2)}) collective-permute-start(bf16[128,1024]{1,0:T(8,128)(2,1)S(1)} %get-tuple-element.31), channel_id=1, source_target_pairs={{0,0},{1,16},{2,2},{3,18},{4,4},{5,20},{6,6},{7,22},{8,8},{9,24},{... | collective-permute-start | bytes 786440 | tf_op jit(solution)/shard_map/ppermute | solution.py:434
  111.1 18.4 %collective-permute-start.14 = (bf16[128,1024]{1,0:T(8,128)(2,1)S(1)}, bf16[128,1024]{1,0:T(8,128)(2,1)S(1)}, u32[]{:S(2)}, u32[]{:S(2)}) collective-permute-start(bf16[128,1024]{1,0:T(8,128)(2,1)S(1)} %get-tuple-element.32), channel_id=1, source_target_pairs={{0,16},{1,0},{2,18},{3,2},{4,20},{5,4},{6,22},{7,6},{8,24},{9,8},{... | collective-permute-start | bytes 786440 | tf_op jit(solution)/shard_map/ppermute | solution.py:434

commit v4 on v3

--- a/solution.py
+++ b/solution.py
@@ -241,19 +241,21 @@
     targets, _, lanes = out_ref.shape
     rows = filter_ref.shape[0]
     reach = taps_ref.shape[1] - 1
-    margin = padded.shape[0] - rows
-    padded[:margin] = jnp.zeros((margin, padded.shape[1]), jnp.float32)
-    edges[...] = jnp.zeros(edges.shape, jnp.float32)
+    margin = padded.shape[1] - rows
+    edges[4 * reach :] = jnp.zeros((edges.shape[0] - 4 * reach, edges.shape[1]), jnp.float32)
+    raw = [qkv_ref[kind].astype(jnp.float32) for kind in (1, 2)]
+    for kind in range(2):
+        padded[kind, :margin] = jnp.zeros((margin, padded.shape[2]), jnp.float32)
+        padded[kind, margin:] = raw[kind]
     mixed_in = None
-    for kind in (1, 2):
-        padded[margin:] = qkv_ref[kind].astype(jnp.float32)
-        feature = taps_ref[kind, 0:1] * padded[margin:]
+    for kind in range(2):
+        feature = taps_ref[kind + 1, 0:1] * raw[kind]
         for tap in range(1, reach + 1):
-            shifted = padded[margin - tap : margin - tap + rows]
-            feature = feature + taps_ref[kind, tap : tap + 1] * shifted
+            shifted = padded[kind, margin - tap : margin - tap + rows]
+            feature = feature + taps_ref[kind + 1, tap : tap + 1] * shifted
         mixed_in = feature if mixed_in is None else mixed_in * feature
-        edges[(kind - 1) * reach : kind * reach] = padded[margin : margin + reach]
-        edges[(kind + 1) * reach : (kind + 2) * reach] = padded[margin + rows - reach :]
+        edges[kind * reach : (kind + 1) * reach] = padded[kind, margin : margin + reach]
+        edges[(kind + 2) * reach : (kind + 3) * reach] = padded[kind, margin + rows - reach :]
     for target in range(targets):
         at = slice(target * lanes, (target + 1) * lanes)
         out_ref[target, :rows] = filter_ref[:, at].astype(out_ref.dtype)
@@ -294,7 +296,7 @@
         ],
         out_specs=pl.BlockSpec((peers // steps, total, lanes), lambda i: (i, 0, 0)),
         scratch_shapes=[
-            pltpu.VMEM((rows + 8, width), jnp.float32),
+            pltpu.VMEM((2, rows + 8, width), jnp.float32),
             pltpu.VMEM((EDGE_ROWS, width), jnp.float32),
         ],
         compiler_params=pltpu.CompilerParams(vmem_limit_bytes=60 * 2**20),

time: 131 us -> 131 us (level)
  no operation moved by 1% of the time
where the time goes in v4:
time: 131 us; the launch traced here: 130 us
  waiting for transfers between devices  77.4 us (59%)
  starting transfers between devices  31.2 us (24%)
  Pallas kernels  17.6 us (13%)
  local copies, waits for them, and re-layouts  4.02 us (3%)
    ppermute x11, waiting for transfers between devices, from_partner(): return lax.ppermute(value, 'ctx', pairs)  40.2 us
    all_to_all x1, waiting for transfers between devices, body(): lax.all_to_all(by_target, 'ctx', split_axis=0, concat_axis=0, tiled=True)  18.9 us
    ppermute x4, waiting for transfers between devices, to_their_place(): return lax.ppermute(partial, ('ctx', 'tp'), pairs)  18.3 us
    ppermute x4, starting transfers between devices, to_their_place(): return lax.ppermute(partial, ('ctx', 'tp'), pairs)  9.88 us
    ppermute x11, starting transfers between devices, from_partner(): return lax.ppermute(value, 'ctx', pairs)  8.08 us
    all_to_all x1, starting transfers between devices, body(): lax.all_to_all(by_target, 'ctx', split_axis=0, concat_axis=0, tiled=True)  6.67 us
    all_to_all x1, starting transfers between devices, body(): lax.all_to_all(packed, 'ctx', split_axis=0, concat_axis=0, tiled=True)  6.62 us
    pallas_call x2, Pallas kernels, project(): pl.pallas_call(functools.partial(project_kernel, [len(parts) for parts in...  6.61 us
  transfers between devices with their start and end apart: 17, of which 10 were waited for; matrix products, arithmetic and copies ran while one was open for 1% of the time, Pallas kernels for 10%

profile of v4, /device:TPU:5, one launch (start us, length us, event | category | flops | bytes accessed | tf_op | source)
XLA Modules:
  0.0 130.4 jit_solution(12644236581089899711)
XLA Ops:
  0.0 0.0 copy-start
  0.0 3.7 %pack.1 = bf16[16,400,128]{2,1,0:T(8,128)(2,1)} custom-call(bf16[3,128,2048]{2,1,0:T(8,128)(2,1)} %bitcast.9, f32[3,3,2048]{2,1,0:T(4,128)} %taps_ref.1, f32[128,2048]{1,0:T(8,128)} %filter_ref.1), custom_call_target="tpu_custom_call" | custom-call | flops 4194304 | bytes 4194304 | tf_op jit(solution)/shard_map/pack/pallas_call | solution.py:288
  3.7 0.0 copy-start.1
  3.7 6.6 %all-to-all-start = ((bf16[16,400,128]{2,1,0:T(8,128)(2,1)}), bf16[16,400,128]{2,1,0:T(8,128)(2,1)}, u32[]{:S(2)}, u32[]{:S(2)}) async-start(bf16[16,400,128]{2,1,0:T(8,128)(2,1)} %pack.1), calls=%async_computation | async-start | bytes 3276800 | tf_op jit(solution)/shard_map/all_to_all | solution.py:457
  10.3 0.0 copy-done.1
  10.3 0.0 copy-start.8
  10.4 1.5 %collective-permute-start.1 = (bf16[896,256]{1,0:T(8,128)(2,1)S(1)}, bf16[896,256]{1,0:T(8,128)(2,1)S(1)}, u32[]{:S(2)}, u32[]{:S(2)}) collective-permute-start(bf16[896,256]{1,0:T(8,128)(2,1)S(1)} %slice.6), channel_id=1, source_target_pairs={{0,8},{2,10},{4,12},{6,14},{8,0},{10,2},{12,4},{14,6},{16,24},{18,... | collective-permute-start | bytes 1376264 | tf_op jit(solution)/shard_map/ppermute | solution.py:381
  11.8 1.2 collective-permute-start
  13.0 0.9 slice.7
  13.9 35.0 %collective-permute-done.1.refs_0_ = bf16[896,256]{1,0:T(8,128)(2,1)S(1)} collective-permute-done((bf16[896,256]{1,0:T(8,128)(2,1)S(1)}, bf16[896,256]{1,0:T(8,128)(2,1)S(1)}, u32[]{:S(2)}, u32[]{:S(2)}) %collective-permute-start.1) | collective-permute-done | bytes 458784 | tf_op jit(solution)/shard_map/ppermute | solution.py:381
  48.9 0.0 copy-start.4
  48.9 0.0 all-to-all-done.arrived_ref
  48.9 0.7 collective-permute-start.2
  49.6 1.4 %collective-permute-start.3 = (bf16[896,256]{1,0:T(8,128)(2,1)S(1)}, bf16[896,256]{1,0:T(8,128)(2,1)}, u32[]{:S(2)}, u32[]{:S(2)}) collective-permute-start(bf16[896,256]{1,0:T(8,128)(2,1)S(1)} %collective-permute-done.1.refs_0_), channel_id=1, source_target_pairs={{0,4},{2,6},{4,0},{6,2},{8,12},{10,14},{12,8},{14,10},{16,20},{18,... | collective-permute-start | bytes 1376264 | tf_op jit(solution)/shard_map/ppermute | solution.py:381
  51.0 0.0 copy-done.8
  51.0 0.0 copy-done
  51.0 0.1 dynamic-slice_bitcast_fusion.skip_ref
  51.1 0.0 copy-start.6
  51.1 1.1 copy-done.6
  52.2 0.0 copy-start.7
  52.2 1.0 copy-done.7
  53.3 6.4 %gated_conv.1 = bf16[2,8,2,128,128]{4,3,2,1,0:T(8,128)(2,1)} custom-call(bf16[512,512]{1,0:T(8,128)(2,1)S(1)} %copy-done.7, bf16[256,1536]{1,0:T(8,128)(2,1)S(1)} %copy-done.6, bf16[16,400,128]{2,1,0:T(8,128)(2,1)} %all-to-all-done.arrived_ref, f32[9,128]{1,0:T(8,128)S(1)} %constant_dynamic-slice_fusion.taps_ref, f32[1,128]{1,0:T(1,128)S(1)} %dynamic-slice_bitcast_fusion.skip_ref), custom_call_target="tpu_custom_call" | custom-call | flops 1879048192 | bytes 5242880 | tf_op jit(solution)/shard_map/gated_conv/pallas_call | solution.py:315
  59.7 0.0 copy-done.4
  59.7 0.0 collective-permute-done.refs_2_
  59.7 3.0 %collective-permute-done.3.refs_4_ = bf16[896,256]{1,0:T(8,128)(2,1)} collective-permute-done((bf16[896,256]{1,0:T(8,128)(2,1)S(1)}, bf16[896,256]{1,0:T(8,128)(2,1)}, u32[]{:S(2)}, u32[]{:S(2)}) %collective-permute-start.3) | collective-permute-done | bytes 458784 | tf_op jit(solution)/shard_map/ppermute | solution.py:381
  62.6 0.5 collective-permute-done.2.refs_1_
  63.1 0.0 copy-start.2
  63.1 0.8 copy-done.2
  63.9 6.7 %all-to-all-start.1 = ((bf16[16,2,128,128]{3,2,1,0:T(8,128)(2,1)}), bf16[16,2,128,128]{3,2,1,0:T(8,128)(2,1)S(1)}, u32[]{:S(2)}, u32[]{:S(2)}) async-start(bf16[16,2,128,128]{3,2,1,0:T(8,128)(2,1)} %bitcast.4), calls=%async_computation.1 | async-start | bytes 2097152 | tf_op jit(solution)/shard_map/all_to_all | solution.py:468
  70.6 0.2 collective-permute-start.4
  70.8 0.3 collective-permute-start.5
  71.1 1.4 %collective-permute-start.10 = (bf16[1152,256]{1,0:T(8,128)(2,1)}, bf16[1152,256]{1,0:T(8,128)(2,1)}, u32[]{:S(2)}, u32[]{:S(2)}) collective-permute-start(bf16[1152,256]{1,0:T(8,128)(2,1)} %copy-done.2), channel_id=1, source_target_pairs={{0,4},{2,6},{4,0},{6,2},{8,12},{10,14},{12,8},{14,10},{16,20},{18,... | collective-permute-start | bytes 1769480 | tf_op jit(solution)/shard_map/ppermute | solution.py:381
  72.5 0.6 collective-permute-start.9
  73.1 0.3 collective-permute-done.4.refs_1_
  73.4 1.5 %collective-permute-done.5.refs_3_ = bf16[2048,256]{1,0:T(8,128)(2,1)} collective-permute-done((bf16[2048,256]{1,0:T(8,128)(2,1)S(1)}, bf16[2048,256]{1,0:T(8,128)(2,1)}, u32[]{:S(2)}, u32[]{:S(2)}) %collective-permute-start.5) | collective-permute-done | bytes 1048608 | tf_op jit(solution)/shard_map/ppermute | solution.py:381
  74.9 18.9 %all-to-all-done.1 = bf16[16,2,128,128]{3,2,1,0:T(8,128)(2,1)S(1)} async-done(((bf16[16,2,128,128]{3,2,1,0:T(8,128)(2,1)}), bf16[16,2,128,128]{3,2,1,0:T(8,128)(2,1)S(1)}, u32[]{:S(2)}, u32[]{:S(2)}) %all-to-all-start.1) | async-done | bytes 1048608 | tf_op jit(solution)/shard_map/all_to_all | solution.py:468
  93.8 0.0 copy-start.5
  93.8 0.0 copy-start.3
  93.8 3.7 %project.2 = (bf16[128,1024]{1,0:T(8,128)(2,1)}, bf16[128,1024]{1,0:T(8,128)(2,1)S(1)}) custom-call(s32[1]{0:T(128)} %bitcast.1.own_ref, bf16[16,256,128]{2,1,0:T(8,128)(2,1)S(1)} %bitcast.7, bf16[2048,256]{1,0:T(8,128)(2,1)S(1)} %copy-done.1, bf16[2048,256]{1,0:T(8,128)(2,1)} %collective-permute-done.4.refs_1_, ...), custom_call_target="tpu_custom_call" | custom-call | flops 1073741824 | bytes 6291456 | tf_op jit(solution)/shard_map/project/pallas_call | solution.py:342
  97.5 0.0 collective-permute-done.10.refs_5_
  97.5 0.3 collective-permute-start.12
  97.8 0.0 copy-done.5
  97.8 0.2 collective-permute-start.8
  98.0 0.3 collective-permute-start.11
  98.3 6.3 %collective-permute-start.6 = (bf16[128,1024]{1,0:T(8,128)(2,1)}, bf16[128,1024]{1,0:T(8,128)(2,1)S(1)}, u32[]{:S(2)}, u32[]{:S(2)}) collective-permute-start(bf16[128,1024]{1,0:T(8,128)(2,1)} %get-tuple-element.25), channel_id=1, source_target_pairs={{0,0},{1,16},{2,2},{3,18},{4,4},{5,20},{6,6},{7,22},{8,8},{9,24},{... | collective-permute-start | bytes 786440 | tf_op jit(solution)/shard_map/ppermute | solution.py:436
  104.6 0.0 collective-permute-done.8.refs_2_
  104.6 0.1 collective-permute-start.7
  104.7 0.0 collective-permute-done.11.refs_6_
  104.7 0.0 collective-permute-done.9.refs_3_
  104.7 0.0 collective-permute-done.12.refs_7_
  104.7 0.0 copy-done.3
  104.8 2.9 %project.3 = (bf16[128,1024]{1,0:T(8,128)(2,1)S(1)}, bf16[128,1024]{1,0:T(8,128)(2,1)S(1)}) custom-call(s32[1]{0:T(128)} %bitcast.1.own_ref, bf16[16,256,128]{2,1,0:T(8,128)(2,1)S(1)} %bitcast.8, bf16[896,256]{1,0:T(8,128)(2,1)S(1)} %copy-done.5, bf16[1152,256]{1,0:T(8,128)(2,1)S(1)} %copy-done.3, bf16[896,256]{1,0:T(8,128)(2,1)S(1)} %collective-permute-done.8.refs_2_, ...), custom_call_target="tpu_custom_call" | custom-call | flops 1073741824 | bytes 6291456 | tf_op jit(solution)/shard_map/project/pallas_call | solution.py:342
  107.6 3.5 %collective-permute-start.13 = (bf16[128,1024]{1,0:T(8,128)(2,1)S(1)}, bf16[128,1024]{1,0:T(8,128)(2,1)S(1)}, u32[]{:S(2)}, u32[]{:S(2)}) collective-permute-start(bf16[128,1024]{1,0:T(8,128)(2,1)S(1)} %get-tuple-element.31), channel_id=1, source_target_pairs={{0,0},{1,16},{2,2},{3,18},{4,4},{5,20},{6,6},{7,22},{8,8},{9,24},{... | collective-permute-start | bytes 786440 | tf_op jit(solution)/shard_map/ppermute | solution.py:436
  111.1 0.1 collective-permute-start.14
  111.2 11.5 %collective-permute-done.6.refs_0_ = bf16[128,1024]{1,0:T(8,128)(2,1)S(1)} collective-permute-done((bf16[128,1024]{1,0:T(8,128)(2,1)}, bf16[128,1024]{1,0:T(8,128)(2,1)S(1)}, u32[]{:S(2)}, u32[]{:S(2)}) %collective-permute-start.6) | collective-permute-done | bytes 262176 | tf_op jit(solution)/shard_map/ppermute | solution.py:436
  122.7 1.2 collective-permute-done.7.refs_1_
  123.9 4.4 %collective-permute-done.13.refs_2_ = bf16[128,1024]{1,0:T(8,128)(2,1)S(1)} collective-permute-done((bf16[128,1024]{1,0:T(8,128)(2,1)S(1)}, bf16[128,1024]{1,0:T(8,128)(2,1)S(1)}, u32[]{:S(2)}, u32[]{:S(2)}) %collective-permute-start.13) | collective-permute-done | bytes 262176 | tf_op jit(solution)/shard_map/ppermute | solution.py:436
  128.3 1.2 collective-permute-done.14.refs_3_
  129.5 0.9 finish.1
  (3 shorter events, 0.1 us)
Async XLA Ops:
  0.0 51.0 %copy-start = (f32[2048]{0:T(1024)S(1)}, f32[2048]{0:T(1024)}, u32[]{:S(2)}) copy-start(f32[2048]{0:T(1024)} %param.10) | copy-start | bytes 24580
  3.7 6.6 %copy-start.1 = (bf16[2048,256]{1,0:T(8,128)(2,1)S(1)}, bf16[2048,256]{1,0:T(8,128)(2,1)}, u32[]{:S(2)}) copy-start(bf16[2048,256]{1,0:T(8,128)(2,1)} %refs_0_) | copy-start | bytes 3145732
  3.7 45.2 %all-to-all-start = ((bf16[16,400,128]{2,1,0:T(8,128)(2,1)}), bf16[16,400,128]{2,1,0:T(8,128)(2,1)}, u32[]{:S(2)}, u32[]{:S(2)}) async-start(bf16[16,400,128]{2,1,0:T(8,128)(2,1)} %pack.1), calls=%async_computation | async-start | bytes 3276800 | tf_op jit(solution)/shard_map/all_to_all | solution.py:457
  10.3 40.6 %copy-start.8 = (f32[3,3,2048]{2,1,0:T(4,128)S(1)}, f32[3,3,2048]{2,1,0:T(4,128)}, u32[]{:S(2)}) copy-start(f32[3,3,2048]{2,1,0:T(4,128)} %taps_ref.1) | copy-start | bytes 221188
  10.4 38.5 %collective-permute-start.1 = (bf16[896,256]{1,0:T(8,128)(2,1)S(1)}, bf16[896,256]{1,0:T(8,128)(2,1)S(1)}, u32[]{:S(2)}, u32[]{:S(2)}) collective-permute-start(bf16[896,256]{1,0:T(8,128)(2,1)S(1)} %slice.6), channel_id=1, source_target_pairs={{0,8},{2,10},{4,12},{6,14},{8,0},{10,2},{12,4},{14,6},{16,24},{18,... | collective-permute-start | bytes 1376264 | tf_op jit(solution)/shard_map/ppermute | solution.py:381
  11.8 47.9 %collective-permute-start = (bf16[2048,256]{1,0:T(8,128)(2,1)S(1)}, bf16[2048,256]{1,0:T(8,128)(2,1)S(1)}, u32[]{:S(2)}, u32[]{:S(2)}) collective-permute-start(bf16[2048,256]{1,0:T(8,128)(2,1)S(1)} %copy-done.1), channel_id=1, source_target_pairs={{0,4},{2,6},{4,0},{6,2},{8,12},{10,14},{12,8},{14,10},{16,20},{18,... | collective-permute-start | bytes 3145736 | tf_op jit(solution)/shard_map/ppermute | solution.py:381
  48.9 10.8 %copy-start.4 = (bf16[896,256]{1,0:T(8,128)(2,1)}, bf16[896,256]{1,0:T(8,128)(2,1)S(1)}, u32[]{:S(2)}) copy-start(bf16[896,256]{1,0:T(8,128)(2,1)S(1)} %collective-permute-done.1.refs_0_) | copy-start | bytes 1376260
  48.9 14.2 %collective-permute-start.2 = (bf16[1152,256]{1,0:T(8,128)(2,1)}, bf16[1152,256]{1,0:T(8,128)(2,1)S(1)}, u32[]{:S(2)}, u32[]{:S(2)}) collective-permute-start(bf16[1152,256]{1,0:T(8,128)(2,1)} %slice.7), channel_id=1, source_target_pairs={{0,8},{2,10},{4,12},{6,14},{8,0},{10,2},{12,4},{14,6},{16,24},{18,... | collective-permute-start | bytes 1769480 | tf_op jit(solution)/shard_map/ppermute | solution.py:381
  49.6 13.1 %collective-permute-start.3 = (bf16[896,256]{1,0:T(8,128)(2,1)S(1)}, bf16[896,256]{1,0:T(8,128)(2,1)}, u32[]{:S(2)}, u32[]{:S(2)}) collective-permute-start(bf16[896,256]{1,0:T(8,128)(2,1)S(1)} %collective-permute-done.1.refs_0_), channel_id=1, source_target_pairs={{0,4},{2,6},{4,0},{6,2},{8,12},{10,14},{12,8},{14,10},{16,20},{18,... | collective-permute-start | bytes 1376264 | tf_op jit(solution)/shard_map/ppermute | solution.py:381
  51.1 1.1 copy-start.6
  52.2 1.0 copy-start.7
  63.1 0.8 copy-start.2
  63.9 29.8 %all-to-all-start.1 = ((bf16[16,2,128,128]{3,2,1,0:T(8,128)(2,1)}), bf16[16,2,128,128]{3,2,1,0:T(8,128)(2,1)S(1)}, u32[]{:S(2)}, u32[]{:S(2)}) async-start(bf16[16,2,128,128]{3,2,1,0:T(8,128)(2,1)} %bitcast.4), calls=%async_computation.1 | async-start | bytes 2097152 | tf_op jit(solution)/shard_map/all_to_all | solution.py:468
  70.6 2.8 %collective-permute-start.4 = (bf16[2048,256]{1,0:T(8,128)(2,1)S(1)}, bf16[2048,256]{1,0:T(8,128)(2,1)}, u32[]{:S(2)}, u32[]{:S(2)}) collective-permute-start(bf16[2048,256]{1,0:T(8,128)(2,1)S(1)} %copy-done.1), channel_id=1, source_target_pairs={{0,2},{2,0},{4,6},{6,4},{8,10},{10,8},{12,14},{14,12},{16,18},{18,... | collective-permute-start | bytes 3145736 | tf_op jit(solution)/shard_map/ppermute | solution.py:381
  70.8 4.1 %collective-permute-start.5 = (bf16[2048,256]{1,0:T(8,128)(2,1)S(1)}, bf16[2048,256]{1,0:T(8,128)(2,1)}, u32[]{:S(2)}, u32[]{:S(2)}) collective-permute-start(bf16[2048,256]{1,0:T(8,128)(2,1)S(1)} %collective-permute-done.refs_2_), channel_id=1, source_target_pairs={{0,2},{2,0},{4,6},{6,4},{8,10},{10,8},{12,14},{14,12},{16,18},{18,... | collective-permute-start | bytes 3145736 | tf_op jit(solution)/shard_map/ppermute | solution.py:381
  71.1 26.4 %collective-permute-start.10 = (bf16[1152,256]{1,0:T(8,128)(2,1)}, bf16[1152,256]{1,0:T(8,128)(2,1)}, u32[]{:S(2)}, u32[]{:S(2)}) collective-permute-start(bf16[1152,256]{1,0:T(8,128)(2,1)} %copy-done.2), channel_id=1, source_target_pairs={{0,4},{2,6},{4,0},{6,2},{8,12},{10,14},{12,8},{14,10},{16,20},{18,... | collective-permute-start | bytes 1769480 | tf_op jit(solution)/shard_map/ppermute | solution.py:381
  72.5 32.2 %collective-permute-start.9 = (bf16[1152,256]{1,0:T(8,128)(2,1)}, bf16[1152,256]{1,0:T(8,128)(2,1)}, u32[]{:S(2)}, u32[]{:S(2)}) collective-permute-start(bf16[1152,256]{1,0:T(8,128)(2,1)} %copy-done.2), channel_id=1, source_target_pairs={{0,2},{2,0},{4,6},{6,4},{8,10},{10,8},{12,14},{14,12},{16,18},{18,... | collective-permute-start | bytes 1769480 | tf_op jit(solution)/shard_map/ppermute | solution.py:381
  93.8 4.1 %copy-start.5 = (bf16[896,256]{1,0:T(8,128)(2,1)S(1)}, bf16[896,256]{1,0:T(8,128)(2,1)}, u32[]{:S(2)}) copy-start(bf16[896,256]{1,0:T(8,128)(2,1)} %copy-done.4) | copy-start | bytes 1376260
  93.8 11.0 %copy-start.3 = (bf16[1152,256]{1,0:T(8,128)(2,1)S(1)}, bf16[1152,256]{1,0:T(8,128)(2,1)}, u32[]{:S(2)}) copy-start(bf16[1152,256]{1,0:T(8,128)(2,1)} %copy-done.2) | copy-start | bytes 1769476
  97.5 7.2 %collective-permute-start.12 = (bf16[1152,256]{1,0:T(8,128)(2,1)}, bf16[1152,256]{1,0:T(8,128)(2,1)S(1)}, u32[]{:S(2)}, u32[]{:S(2)}) collective-permute-start(bf16[1152,256]{1,0:T(8,128)(2,1)} %collective-permute-done.10.refs_5_), channel_id=1, source_target_pairs={{0,2},{2,0},{4,6},{6,4},{8,10},{10,8},{12,14},{14,12},{16,18},{18,... | collective-permute-start | bytes 1769480 | tf_op jit(solution)/shard_map/ppermute | solution.py:381
  97.8 6.8 %collective-permute-start.8 = (bf16[896,256]{1,0:T(8,128)(2,1)S(1)}, bf16[896,256]{1,0:T(8,128)(2,1)S(1)}, u32[]{:S(2)}, u32[]{:S(2)}) collective-permute-start(bf16[896,256]{1,0:T(8,128)(2,1)S(1)} %copy-done.5), channel_id=1, source_target_pairs={{0,2},{2,0},{4,6},{6,4},{8,10},{10,8},{12,14},{14,12},{16,18},{18,... | collective-permute-start | bytes 1376264 | tf_op jit(solution)/shard_map/ppermute | solution.py:381
  98.0 6.7 %collective-permute-start.11 = (bf16[896,256]{1,0:T(8,128)(2,1)}, bf16[896,256]{1,0:T(8,128)(2,1)S(1)}, u32[]{:S(2)}, u32[]{:S(2)}) collective-permute-start(bf16[896,256]{1,0:T(8,128)(2,1)} %collective-permute-done.3.refs_4_), channel_id=1, source_target_pairs={{0,2},{2,0},{4,6},{6,4},{8,10},{10,8},{12,14},{14,12},{16,18},{18,... | collective-permute-start | bytes 1376264 | tf_op jit(solution)/shard_map/ppermute | solution.py:381
  98.3 24.3 %collective-permute-start.6 = (bf16[128,1024]{1,0:T(8,128)(2,1)}, bf16[128,1024]{1,0:T(8,128)(2,1)S(1)}, u32[]{:S(2)}, u32[]{:S(2)}) collective-permute-start(bf16[128,1024]{1,0:T(8,128)(2,1)} %get-tuple-element.25), channel_id=1, source_target_pairs={{0,0},{1,16},{2,2},{3,18},{4,4},{5,20},{6,6},{7,22},{8,8},{9,24},{... | collective-permute-start | bytes 786440 | tf_op jit(solution)/shard_map/ppermute | solution.py:436
  104.6 19.2 %collective-permute-start.7 = (bf16[128,1024]{1,0:T(8,128)(2,1)S(1)}, bf16[128,1024]{1,0:T(8,128)(2,1)S(1)}, u32[]{:S(2)}, u32[]{:S(2)}) collective-permute-start(bf16[128,1024]{1,0:T(8,128)(2,1)S(1)} %get-tuple-element.26), channel_id=1, source_target_pairs={{0,16},{1,0},{2,18},{3,2},{4,20},{5,4},{6,22},{7,6},{8,24},{9,8},{... | collective-permute-start | bytes 786440 | tf_op jit(solution)/shard_map/ppermute | solution.py:436
  107.6 20.7 %collective-permute-start.13 = (bf16[128,1024]{1,0:T(8,128)(2,1)S(1)}, bf16[128,1024]{1,0:T(8,128)(2,1)S(1)}, u32[]{:S(2)}, u32[]{:S(2)}) collective-permute-start(bf16[128,1024]{1,0:T(8,128)(2,1)S(1)} %get-tuple-element.31), channel_id=1, source_target_pairs={{0,0},{1,16},{2,2},{3,18},{4,4},{5,20},{6,6},{7,22},{8,8},{9,24},{... | collective-permute-start | bytes 786440 | tf_op jit(solution)/shard_map/ppermute | solution.py:436
  111.1 18.4 %collective-permute-start.14 = (bf16[128,1024]{1,0:T(8,128)(2,1)S(1)}, bf16[128,1024]{1,0:T(8,128)(2,1)S(1)}, u32[]{:S(2)}, u32[]{:S(2)}) collective-permute-start(bf16[128,1024]{1,0:T(8,128)(2,1)S(1)} %get-tuple-element.32), channel_id=1, source_target_pairs={{0,16},{1,0},{2,18},{3,2},{4,20},{5,4},{6,22},{7,6},{8,24},{9,8},{... | collective-permute-start | bytes 786440 | tf_op jit(solution)/shard_map/ppermute | solution.py:436
